TPU v7x, 32 devices: a whole 2x2x4 slice. The times are simulated.
32 devices in a mesh: lev: 2 (over y), tile: 16 (over z, x, core).
Axes of the slice: x: 2, y: 2, z: 4, core: 2. Of those that a mesh axis runs over, the one named last changes fastest.
Arguments:
- prognostic: float32 [4, 128, 131072], P(None, 'lev', 'tile'), may hold values from -6 to 6
- neighbours: int32 [4, 131072], P(None, 'tile'), may hold values from 0 to 8447, as said below
- metric: float32 [2, 4, 131072], P(None, None, 'tile'), may hold values from -0.9 to 0.9
- inverses: float32 [16, 128, 128], P('tile')
Outputs:
- advanced: float32 [4, 128, 131072], P(None, 'lev', 'tile')
Inputs may be any that keep to these rules, and one draw needn't show every extreme that they name: `neighbours`: entry [k, c] indexes the cells of c's tile extended by 128 cells on each side: 0 to 127 are the last 128 cells of the previous tile, then the tile's own 8192 cells in order, then the first 128 cells of the next tile, the tiles forming a closed cycle; each entry lies within 128 of 128 + (c mod 8192).
All inputs are finite; a program needn't handle non-finite values.
Results may differ from a plain program's by a relative error of at most 0.0001.
Values sent between devices are 32-bit elements; how exact they have to be, the bound alone decides.
No kernel may reach another device: no remote copies, remote signals or barrier semaphores. Data moves between devices by JAX's collectives and lax.ppermute only.
A program may use at most 128 MiB of HBM per device.

v0:
```python
import functools

import jax
import jax.numpy as jnp
from jax import lax
from jax.experimental import pallas as pl
from jax.experimental.pallas import tpu as pltpu
from jax.sharding import PartitionSpec as P

HALO = 128
LANES = 128
BLOCK = 256
SUBSTEPS = 3
CHUNKS = 8
LAG = 4
EARLY = 6
UNROLL = 1
EDGE_LAG = 2
VMEM_LIMIT = 5 * 2**20

acoustic = 0.4
half_acoustic = 0.5 * acoustic

f32 = jnp.float32
bf16 = jnp.bfloat16


def dot(a, b):
    return jnp.dot(a, b, preferred_element_type=f32)


def exact_dot(a, b):
    return jnp.dot(a, b, preferred_element_type=f32, precision=lax.Precision.HIGHEST)


def split(x):
    hi = x.astype(bf16)
    return hi, (x - hi.astype(f32)).astype(bf16)


def aligned(x, to):
    return x if isinstance(x, int) else pl.multiple_of(x, to)


class Plan:
    def __init__(self, groups, levels, cells, directions):
        self.groups = groups
        self.levels = levels
        self.cells = cells
        self.directions = directions
        self.total = groups * levels
        self.chunks = CHUNKS
        self.width = cells // CHUNKS
        self.extras = 1 if groups == 2 else 2
        self.rows = -(-(self.total + self.extras * groups) // 16) * 16
        self.pieces = self.width // LANES
        self.sent = (levels + self.extras) * self.pieces
        self.slots = self.schedule()

    def schedule(self):
        chunks = self.chunks
        slots = [(0, (1 + q) % chunks) for q in range(chunks)]
        for substep in range(1, SUBSTEPS):
            done = {c: t + LAG for t, (s, c) in enumerate(slots) if s == substep - 1}
            ready = {}
            for c in range(chunks):
                at_edge = c in (0, chunks - 1)
                near = [done[d % chunks] + (EDGE_LAG if at_edge and not 0 <= d < chunks else 0) for d in (c - 1, c, c + 1)]
                ready[c] = (max(near), not at_edge)
            left = set(range(chunks))
            while left:
                now = [c for c in left if ready[c][0] <= len(slots)] or left
                c = min(now, key=lambda c: (ready[c][1], ready[c][0], c) if now is not left else (ready[c][0], c))
                left.remove(c)
                slots.append((substep, c))
        return slots


def operator(plan, me, inverse_ref, g_ref):
    levels, total, groups, rows = plan.levels, plan.total, plan.groups, plan.rows
    extras = plan.extras
    r = lax.broadcasted_iota(jnp.int32, (rows, total), 0)
    c = lax.broadcasted_iota(jnp.int32, (rows, total), 1)

    def wrapped(x):
        return jnp.where(x >= groups, x - groups, x)

    wanted = jnp.full((rows, total), -1, jnp.int32)
    for shift in range(groups):
        to = wrapped(me + shift)
        wanted = jnp.where((r >= shift * levels) & (r < (shift + 1) * levels), r - shift * levels + to * levels, wanted)
        first = total + shift * extras
        if groups == 2:
            edge = jnp.where(to == 0, levels, levels - 1)
            wanted = jnp.where(r == first, edge, wanted)
        else:
            wanted = jnp.where(r == first, to * levels - 1, wanted)
            wanted = jnp.where(r == first + 1, (to + 1) * levels, wanted)
    pick = (wanted == c).astype(f32)
    row = lax.broadcasted_iota(jnp.int32, (total, 2 * levels), 0)
    col = lax.broadcasted_iota(jnp.int32, (total, 2 * levels), 1)
    own = me * levels + jnp.where(col >= levels, col - levels, col)
    slope = jnp.where(row == own - 1, -half_acoustic, 0.0) + jnp.where(row == own + 1, half_acoustic, 0.0)
    mix = jnp.where(col < levels, jnp.where(row == own, 1.0, 0.0), slope)
    g = exact_dot(exact_dot(pick, inverse_ref[...]), mix)
    hi, lo = split(g)
    g_ref[0:rows, :] = hi
    g_ref[rows : 2 * rows, :] = lo


def correct(plan, me, fields, x_ref, chunk, got):
    levels, pieces = plan.levels, plan.pieces
    row = lax.broadcasted_iota(jnp.int32, (levels, LANES), 0)
    for j in range(pieces):
        cols = pl.ds(chunk * plan.width + j * LANES, LANES)
        v = fields[3, :, cols]
        for g in got:
            v = v + g[j * levels : (j + 1) * levels, :]
        x = []
        for e in range(plan.extras):
            at = levels * pieces + e * pieces + j
            one = x_ref[e : e + 1, cols]
            for g in got:
                one = one + g[at : at + 1, :]
            x.append(one)
        if plan.groups == 2:
            below = jnp.where(me == 0, 0.0, x[0])
            above = jnp.where(me == 0, x[0], 0.0)
        else:
            below, above = x
        down = jnp.where(row == 0, below, pltpu.roll(v, 1, 0))
        up = jnp.where(row == levels - 1, above, pltpu.roll(v, levels - 1, 0))
        fields[2, :, cols] = fields[2, :, cols] - half_acoustic * (up - down)
        fields[3, :, cols] = v


def weights(plan, start, first, near_ref, metric_ref, m_ref, sum_ref):
    span = BLOCK + 2 * HALO
    tall = 16
    cols = pl.ds(first, BLOCK)
    directions = range(plan.directions)
    local = [near_ref[k : k + 1, cols] - (start + first) for k in directions]
    index = [jnp.broadcast_to(x, (tall, BLOCK)).astype(jnp.int16) for x in local]
    parts = []
    for which in range(2):
        w = [metric_ref[which, k : k + 1, cols] for k in directions]
        sum_ref[which : which + 1, cols] = functools.reduce(jnp.add, w)
        joined = []
        for k in directions:
            x = w[k]
            for j in range(k + 1, plan.directions):
                x = x + jnp.where(local[j] == local[k], w[j], 0.0)
            joined.append(jnp.broadcast_to(x, (tall, BLOCK)))
        pairs = [split(x) for x in joined]
        parts.append([p[0] for p in pairs])
        parts.append([p[1] for p in pairs])
    row = lax.broadcasted_iota(jnp.int32, (tall, BLOCK), 0).astype(jnp.int16)
    zero = jnp.zeros((tall, BLOCK), bf16)
    for r in range(0, span, tall):
        slot = row + jnp.int16(r)
        hits = [slot == index[k] for k in directions]
        for i, values in enumerate(parts):
            x = zero
            for k in reversed(directions):
                x = jnp.where(hits[k], values[k], x)
            m_ref[i, r : r + tall, :] = x


def advance(plan, pieces, src, origin, new, start, m, build, sum_ref, g_ref, f, x_ref, sends):
    levels, width = plan.levels, plan.width
    span = BLOCK + 2 * HALO
    blocks = width // BLOCK
    for ref, col, into, count in pieces:
        there = pl.ds(into, count)
        for field, places in ((0, ((1,), (0,))), (1, ((6,), (7,))), (2, ((2, 5), (3, 4)))):
            for part, rows in zip(split(ref[field, :, pl.ds(col, count)]), places):
                for at in rows:
                    f[at * levels : (at + 1) * levels, there] = part

    def block(b, carry):
        first = aligned(b * BLOCK, BLOCK)
        if build is not None and b > 0:
            build(first, m.at[b])
        cols = pl.ds(first, BLOCK)
        mine = pl.ds(aligned(origin + first, LANES), BLOCK)
        into = pl.ds(aligned(start + first, BLOCK), BLOCK)
        wide = pl.ds(first, span)
        eh = dot(f[0 : 4 * levels, wide], m[b, 0])
        el = dot(f[levels : 3 * levels, wide], m[b, 1])
        nh = dot(f[4 * levels : 8 * levels, wide], m[b, 2])
        nl = dot(f[5 * levels : 7 * levels, wide], m[b, 3])

        def rows(x, i):
            return x[i * levels : (i + 1) * levels]

        ue = rows(eh, 0) + rows(eh, 1) + rows(el, 0)
        pe = rows(eh, 2) + rows(eh, 3) + rows(el, 1)
        pn = rows(nh, 0) + rows(nh, 1) + rows(nl, 0)
        vn = rows(nh, 2) + rows(nh, 3) + rows(nl, 1)
        se, sn = sum_ref[0:1, cols], sum_ref[1:2, cols]
        u, v, p = src[0, :, mine], src[1, :, mine], src[2, :, mine]
        new[0, :, into] = u - (pe - se * p)
        new[1, :, into] = v - (pn - sn * p)
        pressure = p - ((ue - se * u) + (vn - sn * v))
        new[2, :, into] = pressure
        z_hi, z_lo = split(jnp.concatenate([src[3, :, mine], pressure], axis=0))
        y2 = dot(g_ref[...], z_hi)
        y = y2[: plan.rows] + y2[plan.rows :] + dot(g_ref[0 : plan.rows, :], z_lo)
        new[3, :, into] = y[:levels]
        x_ref[:, into] = y[plan.total : plan.total + 8]
        for s, send in enumerate(sends):
            for i in range(BLOCK // LANES):
                part = slice(i * LANES, (i + 1) * LANES)
                j = b * (BLOCK // LANES) + i
                send[pl.ds(aligned(j * levels, 8), levels), :] = y[(s + 1) * levels : (s + 2) * levels, part]
                for e in range(plan.extras):
                    at = plan.total + (s + 1) * plan.extras + e
                    send[pl.ds(levels * plan.pieces + e * plan.pieces + j, 1), :] = y[at : at + 1, part]
        return carry

    if build is None:
        lax.fori_loop(0, blocks, block, 0, unroll=UNROLL)
    else:
        for b in range(blocks):
            block(b, 0)


FAR = ("prognostic", "inverse", "near", "metric", "result")


def call(plan, arrays, outs, aliased, chunk=None, fixes=(), setup=False):
    groups, levels, cells, width, chunks = plan.groups, plan.levels, plan.cells, plan.width, plan.chunks
    in_names, out_names = list(arrays), list(outs)
    fresh = "prognostic" in arrays

    scratch = {}
    if chunk is not None:
        scratch["f"] = pltpu.VMEM((8 * levels, width + 2 * HALO), bf16)
    if fresh:
        scratch["win"] = pltpu.VMEM((4, levels, width + 2 * HALO), f32)
        scratch["near_v"] = pltpu.VMEM((plan.directions, width), jnp.int32)
        scratch["met_v"] = pltpu.VMEM((2, plan.directions, width), f32)
    if setup:
        scratch["inv_v"] = pltpu.VMEM((plan.total, plan.total), f32)
    scratch["sems"] = pltpu.SemaphoreType.DMA((8,))
    scratch_names = list(scratch)

    def kernel(*refs):
        r = dict(zip(in_names, refs))
        r.update(zip(out_names, refs[len(in_names) :]))
        r.update(zip(scratch_names, refs[len(in_names) + len(out_names) :]))
        used = [0]

        def copy(src, dst):
            c = pltpu.make_async_copy(src, dst, r["sems"].at[used[0]])
            used[0] += 1
            c.start()
            return c

        who = r["me"][0]
        stores = []
        if fresh:
            start = chunk * width
            lo = start if chunk == 0 else start - HALO
            hi = start + width if chunk == chunks - 1 else start + width + HALO
            into = lo - (start - HALO)
            near = pl.ds(start, width)
            loads = [copy(r["near"].at[:, near], r["near_v"]), copy(r["metric"].at[:, :, near], r["met_v"])]
            if setup:
                loads.append(copy(r["inverse"], r["inv_v"]))
            late = copy(r["prognostic"].at[:, :, pl.ds(lo, hi - lo)], r["win"].at[:, :, pl.ds(into, hi - lo)])
            for c in loads:
                c.wait()
            if setup:
                operator(plan, who, r["inv_v"], r["g"])
        for name, b in fixes:
            at = pl.ds(b * width, width)
            got = [r[f"got_{name}{b}_{s}"] for s in range(groups - 1)]
            if "result" in r:
                stores.append(copy(r[name].at[0:2, :, at], r["result"].at[0:2, :, at]))
            correct(plan, who, r[name], r[f"{name}_x"], b, got)
            if "result" in r:
                stores.append(copy(r[name].at[2:4, :, at], r["result"].at[2:4, :, at]))
            if b == 0 and "edge_low" in r:
                r["edge_low"][...] = r[name][0:3, :, 0:HALO]
            if b == chunks - 1 and "edge_high" in r:
                r["edge_high"][...] = r[name][0:3, :, cells - HALO : cells]
        if chunk is not None:
            start = chunk * width
            src, origin = (r["win"], HALO) if fresh else (r["old"], start)
            lo = origin if chunk == 0 else origin - HALO
            hi = origin + width if chunk == chunks - 1 else origin + width + HALO
            pieces = [(src, lo, lo - (origin - HALO), hi - lo)]
            if chunk == 0:
                pieces.append((r["halo_low"], 0, 0, HALO))
            if chunk == chunks - 1:
                pieces.append((r["halo_high"], 0, width + HALO, HALO))
            sends = [r[f"send{s}"] for s in range(groups - 1)]
            build = None
            if fresh:

                def build(first, m):
                    weights(plan, start, first, r["near_v"], r["met_v"], m, r["sums"])

            if fresh:
                build(0, r["m"].at[0])
                late.wait()
            advance(
                plan, pieces, src, origin, r["new"], start, r["m"], build, r["sums"], r["g"], r["f"], r["new_x"], sends
            )
        for c in stores:
            c.wait()

    def spec(name):
        if name == "me":
            return pl.BlockSpec(memory_space=pltpu.SMEM)
        return pl.BlockSpec(memory_space=pltpu.HBM if name in FAR else pltpu.VMEM)

    def shape(name):
        s = outs[name]
        return (pltpu.HBM if name in FAR else pltpu.VMEM)(s.shape, s.dtype)

    def placed(name, x):
        if name == "me":
            return x
        return pltpu.with_memory_space_constraint(x, pltpu.HBM if name in FAR else pltpu.VMEM)

    results = pl.pallas_call(
        kernel,
        out_shape=[shape(name) for name in out_names],
        in_specs=[spec(name) for name in in_names],
        out_specs=[spec(name) for name in out_names],
        scratch_shapes=list(scratch.values()),
        input_output_aliases={in_names.index(name): out_names.index(name) for name in aliased},
        cost_estimate=pl.CostEstimate(flops=0, bytes_accessed=0, transcendentals=0),
        compiler_params=pltpu.CompilerParams(vmem_limit_bytes=VMEM_LIMIT),
        name=f"advance_{chunk}" if chunk is not None else "complete",
    )(*[placed(name, x) for name, x in arrays.items()])
    return dict(zip(out_names, results))


def per_device(prognostic, neighbours, metric, inverses):
    groups = lax.axis_size("lev")
    tiles = lax.axis_size("tile")
    levels, cells = prognostic.shape[1:]
    plan = Plan(groups, levels, cells, neighbours.shape[0])
    me = lax.axis_index("lev").astype(jnp.int32).reshape(1)

    def shape(dims, dtype=f32):
        return jax.ShapeDtypeStruct(dims, dtype)

    def shifted(x, by):
        return lax.ppermute(x, "lev", [(i, (i + by) % groups) for i in range(groups)])

    def from_low(x):
        return lax.ppermute(x, "tile", [(i, (i + 1) % tiles) for i in range(tiles)])

    def from_high(x):
        return lax.ppermute(x, "tile", [((i + 1) % tiles, i) for i in range(tiles)])

    halo_low = from_low(prognostic[0:3, :, cells - HALO :])
    halo_high = from_high(prognostic[0:3, :, :HALO])
    last = plan.chunks - 1
    state = {}
    kept, got = {}, {}
    g = result = None
    fixed = set()
    for slot in range(len(plan.slots) + LAG):
        substep, chunk = plan.slots[slot] if slot < len(plan.slots) else (SUBSTEPS - 1, None)
        due = [x for x in plan.slots[: max(slot - LAG + 1, 0)] if x not in fixed]
        if chunk is not None and substep > 0:
            due += [(substep - 1, c) for c in (chunk - 1, chunk, chunk + 1) if 0 <= c <= last and (substep - 1, c) not in fixed]
        due = list(dict.fromkeys(due))
        fixed.update(due)
        names = {substep: "new", substep - 1: "old"}
        arrays, outs, aliased = dict(me=me), {}, []
        for s in sorted({x[0] for x in due} | ({substep, substep - 1} if chunk is not None else set())):
            if s < 0:
                continue
            name = names[s]
            written = s == substep and chunk is not None
            if s in state:
                arrays[name], arrays[f"{name}_x"] = state[s]
            if written or any(x[0] == s for x in due):
                outs[name] = shape(prognostic.shape)
                if s in state:
                    aliased.append(name)
            if written:
                outs[f"{name}_x"] = shape((8, cells))
                if s in state:
                    aliased.append(f"{name}_x")
        for x in due:
            for i in range(groups - 1):
                arrays[f"got_{names[x[0]]}{x[1]}_{i}"] = got[x][i]
            if x[0] < SUBSTEPS - 1 and x[1] in (0, last):
                outs["edge_low" if x[1] == 0 else "edge_high"] = shape((3, levels, HALO))
            if x[0] == SUBSTEPS - 1 and "result" not in outs:
                outs["result"] = shape(prognostic.shape)
                if result is not None:
                    arrays["result"] = result
                    aliased.append("result")
        setup = g is None
        if chunk is not None:
            if substep == 0:
                arrays.update(prognostic=prognostic, near=neighbours, metric=metric)
                outs["m"] = shape((plan.width // BLOCK, 4, BLOCK + 2 * HALO, BLOCK), dtype=bf16)
                outs["sums"] = shape((8, plan.width))
            else:
                arrays.update(m=kept[chunk][0], sums=kept[chunk][1])
            early = slot == EARLY
            if chunk == 0 or early:
                arrays["halo_low"] = halo_low
            if chunk == last or early:
                arrays["halo_high"] = halo_high
            if setup:
                arrays["inverse"] = inverses[0]
                outs["g"] = shape((2 * plan.rows, 2 * levels), dtype=bf16)
            else:
                arrays["g"] = g
            for i in range(groups - 1):
                outs[f"send{i}"] = shape((plan.sent, LANES))
        fixes = [(names[s], c) for s, c in due]
        res = call(plan, arrays, outs, aliased, chunk=chunk, fixes=fixes, setup=setup)
        g = res.get("g", g)
        result = res.get("result", result)
        for s, name in names.items():
            if name in res:
                state[s] = res[name], res.get(f"{name}_x", state[s][1] if s in state else None)
        if chunk is not None:
            if substep == 0:
                kept[chunk] = res["m"], res["sums"]
            got[substep, chunk] = [shifted(res[f"send{i}"], i + 1) for i in range(groups - 1)]
        if "edge_high" in res:
            halo_low = from_low(res["edge_high"])
        if "edge_low" in res:
            halo_high = from_high(res["edge_low"])
    return result


def solution(mesh):
    in_specs = (
        P(None, "lev", "tile"),
        P(None, "tile"),
        P(None, None, "tile"),
        P("tile", None, None),
    )
    out_specs = P(None, "lev", "tile")
    return jax.shard_map(
        per_device, mesh=mesh, in_specs=in_specs, out_specs=out_specs, check_vma=False
    )
```

profile of v0, /device:TPU:0, one launch (start us, length us, event | category | flops | bytes accessed | tf_op | source)
XLA Modules:
  0.0 147.5 jit_solution(7021409229265069834)
XLA Ops:
  0.0 3.8 %advance_1.3 = (f32[4,64,8192]{2,1,0:T(8,128)S(1)}, f32[8,8192]{1,0:T(8,128)S(1)}, bf16[4,4,512,256]{3,2,1,0:T(8,128)(2,1)S(1)}, f32[8,1024]{1,0:T(8,128)S(1)}, ...) custom-call(s32[1]{0:T(128)} %bitcast.refs_0_, f32[4,64,8192]{2,1,0:T(8,128)} %refs_4_.13, s32[4,8192]{1,0:T(4,128)} %refs_5_.13, ...), custom_call_target="tpu_custom_call" | custom-call | tf_op jit(solution)/shard_map/advance_1/pallas_call | solution.py:328
  3.8 3.0 %collective-permute-start = (f32[520,128]{1,0:T(8,128)S(1)}, f32[520,128]{1,0:T(8,128)S(1)}, u32[]{:S(2)}, u32[]{:S(2)}) collective-permute-start(f32[520,128]{1,0:T(8,128)S(1)} %get-tuple-element.126), channel_id=1, source_target_pairs={{0,16},{16,0},{1,17},{17,1},{2,18},{18,2},{3,19},{19,3},{4,20},{20... | collective-permute-start | bytes 798728 | tf_op jit(solution)/shard_map/ppermute | solution.py:353
  6.8 3.5 %advance_2.3 = (f32[4,64,8192]{2,1,0:T(8,128)S(1)}, f32[8,8192]{1,0:T(8,128)S(1)}, bf16[4,4,512,256]{3,2,1,0:T(8,128)(2,1)S(1)}, f32[8,1024]{1,0:T(8,128)S(1)}, f32[520,128]{1,0:T(8,128)S(1)}) custom-call(s32[1]{0:T(128)} %bitcast.refs_0_, f32[4,64,8192]{2,1,0:T(8,128)S(1)} %get-tuple-element.117.refs_1_, ...), custom_call_target="tpu_custom_call", output_to_operand_aliasing={{0}: (1, {}), {1}: (2, {})} | custom-call | tf_op jit(solution)/shard_map/advance_2/pallas_call | solution.py:328
  10.4 2.0 %copy-done.2 = bf16[4,4,512,256]{3,2,1,0:T(8,128)(2,1)} copy-done((bf16[4,4,512,256]{3,2,1,0:T(8,128)(2,1)}, bf16[4,4,512,256]{3,2,1,0:T(8,128)(2,1)S(1)}, u32[]{:S(2)}) %copy-start.2) | copy-done | bytes 4194328
  12.4 3.5 %advance_3.3 = (f32[4,64,8192]{2,1,0:T(8,128)S(1)}, f32[8,8192]{1,0:T(8,128)S(1)}, bf16[4,4,512,256]{3,2,1,0:T(8,128)(2,1)S(1)}, f32[8,1024]{1,0:T(8,128)S(1)}, f32[520,128]{1,0:T(8,128)S(1)}) custom-call(s32[1]{0:T(128)} %bitcast.refs_0_, f32[4,64,8192]{2,1,0:T(8,128)S(1)} %get-tuple-element.120.refs_1_, ...), custom_call_target="tpu_custom_call", output_to_operand_aliasing={{0}: (1, {}), {1}: (2, {})} | custom-call | tf_op jit(solution)/shard_map/advance_3/pallas_call | solution.py:328
  15.9 2.1 %collective-permute-start.2 = (f32[520,128]{1,0:T(8,128)S(1)}, f32[520,128]{1,0:T(8,128)S(1)}, u32[]{:S(2)}, u32[]{:S(2)}) collective-permute-start(f32[520,128]{1,0:T(8,128)S(1)} %get-tuple-element.132), channel_id=1, source_target_pairs={{0,16},{16,0},{1,17},{17,1},{2,18},{18,2},{3,19},{19,3},{4,20},{20... | collective-permute-start | bytes 798728 | tf_op jit(solution)/shard_map/ppermute | solution.py:353
  18.0 3.5 %advance_4.3 = (f32[4,64,8192]{2,1,0:T(8,128)S(1)}, f32[8,8192]{1,0:T(8,128)S(1)}, bf16[4,4,512,256]{3,2,1,0:T(8,128)(2,1)S(1)}, f32[8,1024]{1,0:T(8,128)S(1)}, f32[520,128]{1,0:T(8,128)S(1)}) custom-call(s32[1]{0:T(128)} %bitcast.refs_0_, f32[4,64,8192]{2,1,0:T(8,128)S(1)} %get-tuple-element.122.refs_1_, ...), custom_call_target="tpu_custom_call", output_to_operand_aliasing={{0}: (1, {}), {1}: (2, {})} | custom-call | tf_op jit(solution)/shard_map/advance_4/pallas_call | solution.py:328
  21.6 1.1 collective-permute-start.5
  22.7 1.0 fusion
  23.7 3.4 %collective-permute-start.4 = (f32[3,64,128]{2,1,0:T(8,128)S(1)}, f32[3,64,128]{2,1,0:T(8,128)S(1)}, u32[]{:S(2)}, u32[]{:S(2)}) collective-permute-start(f32[3,64,128]{2,1,0:T(8,128)S(1)} %get-tuple-element.229), channel_id=1, source_target_pairs={{1,0},{2,1},{3,2},{4,3},{5,4},{6,5},{7,6},{8,7},{9,8},{10,9},{11,1... | collective-permute-start | bytes 294920 | tf_op jit(solution)/shard_map/ppermute | solution.py:359
  27.1 3.5 %advance_5.3 = (f32[4,64,8192]{2,1,0:T(8,128)S(1)}, f32[8,8192]{1,0:T(8,128)S(1)}, bf16[4,4,512,256]{3,2,1,0:T(8,128)(2,1)S(1)}, f32[8,1024]{1,0:T(8,128)S(1)}, f32[520,128]{1,0:T(8,128)S(1)}) custom-call(s32[1]{0:T(128)} %bitcast.refs_0_, f32[4,64,8192]{2,1,0:T(8,128)S(1)} %get-tuple-element.124.refs_1_, ...), custom_call_target="tpu_custom_call", output_to_operand_aliasing={{0}: (1, {}), {1}: (2, {})} | custom-call | tf_op jit(solution)/shard_map/advance_5/pallas_call | solution.py:328
  30.6 0.6 collective-permute-start.6
  31.2 3.5 %advance_6.3 = (f32[4,64,8192]{2,1,0:T(8,128)S(1)}, f32[8,8192]{1,0:T(8,128)S(1)}, bf16[4,4,512,256]{3,2,1,0:T(8,128)(2,1)S(1)}, f32[8,1024]{1,0:T(8,128)S(1)}, f32[520,128]{1,0:T(8,128)S(1)}) custom-call(s32[1]{0:T(128)} %bitcast.refs_0_, f32[4,64,8192]{2,1,0:T(8,128)S(1)} %get-tuple-element.127.refs_1_, ...), custom_call_target="tpu_custom_call", output_to_operand_aliasing={{0}: (1, {}), {1}: (2, {})} | custom-call | tf_op jit(solution)/shard_map/advance_6/pallas_call | solution.py:328
  34.8 1.5 %collective-permute-start.7 = (f32[520,128]{1,0:T(8,128)S(1)}, f32[520,128]{1,0:T(8,128)S(1)}, u32[]{:S(2)}, u32[]{:S(2)}) collective-permute-start(f32[520,128]{1,0:T(8,128)S(1)} %get-tuple-element.144), channel_id=1, source_target_pairs={{0,16},{16,0},{1,17},{17,1},{2,18},{18,2},{3,19},{19,3},{4,20},{20... | collective-permute-start | bytes 798728 | tf_op jit(solution)/shard_map/ppermute | solution.py:353
  36.3 3.5 %advance_7.3 = (f32[4,64,8192]{2,1,0:T(8,128)S(1)}, f32[8,8192]{1,0:T(8,128)S(1)}, bf16[4,4,512,256]{3,2,1,0:T(8,128)(2,1)S(1)}, f32[8,1024]{1,0:T(8,128)S(1)}, f32[520,128]{1,0:T(8,128)S(1)}) custom-call(s32[1]{0:T(128)} %bitcast.refs_0_, f32[4,64,8192]{2,1,0:T(8,128)S(1)} %get-tuple-element.130.refs_1_, ...), custom_call_target="tpu_custom_call", output_to_operand_aliasing={{0}: (1, {}), {1}: (2, {})} | custom-call | tf_op jit(solution)/shard_map/advance_7/pallas_call | solution.py:328
  39.8 0.6 collective-permute-start.8
  40.5 3.5 %advance_0.3 = (f32[4,64,8192]{2,1,0:T(8,128)S(1)}, f32[8,8192]{1,0:T(8,128)S(1)}, bf16[4,4,512,256]{3,2,1,0:T(8,128)(2,1)S(1)}, f32[8,1024]{1,0:T(8,128)S(1)}, f32[520,128]{1,0:T(8,128)S(1)}) custom-call(s32[1]{0:T(128)} %bitcast.refs_0_, f32[4,64,8192]{2,1,0:T(8,128)S(1)} %get-tuple-element.133.refs_1_, ...), custom_call_target="tpu_custom_call", output_to_operand_aliasing={{0}: (1, {}), {1}: (2, {})} | custom-call | tf_op jit(solution)/shard_map/advance_0/pallas_call | solution.py:328
  44.0 1.5 %collective-permute-start.9 = (f32[520,128]{1,0:T(8,128)S(1)}, f32[520,128]{1,0:T(8,128)S(1)}, u32[]{:S(2)}, u32[]{:S(2)}) collective-permute-start(f32[520,128]{1,0:T(8,128)S(1)} %get-tuple-element.156), channel_id=1, source_target_pairs={{0,16},{16,0},{1,17},{17,1},{2,18},{18,2},{3,19},{19,3},{4,20},{20... | collective-permute-start | bytes 798728 | tf_op jit(solution)/shard_map/ppermute | solution.py:353
  45.6 2.2 %copy-done.3 = bf16[4,4,512,256]{3,2,1,0:T(8,128)(2,1)S(1)} copy-done((bf16[4,4,512,256]{3,2,1,0:T(8,128)(2,1)S(1)}, bf16[4,4,512,256]{3,2,1,0:T(8,128)(2,1)}, u32[]{:S(2)}) %copy-start.3) | copy-done | bytes 4194328
  47.7 2.6 %advance_2.4 = (f32[4,64,8192]{2,1,0:T(8,128)S(1)}, f32[4,64,8192]{2,1,0:T(8,128)S(1)}, f32[8,8192]{1,0:T(8,128)S(1)}, f32[520,128]{1,0:T(8,128)S(1)}) custom-call(s32[1]{0:T(128)} %bitcast.refs_0_, f32[4,64,8192]{2,1,0:T(8,128)S(1)} %get-tuple-element.136.refs_1_, f32[8,8192]{1,0:T(8,128)S(1)} %get-tuple-element.137.refs_2_, ...), custom_call_target="tpu_custom_call", output_to_operand_aliasing={{0}: (1, {})} | custom-call | tf_op jit(solution)/shard_map/advance_2/pallas_call | solution.py:328
  50.4 1.0 collective-permute-start.10
  51.3 2.6 %advance_3.4 = (f32[4,64,8192]{2,1,0:T(8,128)S(1)}, f32[4,64,8192]{2,1,0:T(8,128)S(1)}, f32[8,8192]{1,0:T(8,128)S(1)}, f32[520,128]{1,0:T(8,128)S(1)}) custom-call(s32[1]{0:T(128)} %bitcast.refs_0_, f32[4,64,8192]{2,1,0:T(8,128)S(1)} %get-tuple-element.141.refs_1_, ...), custom_call_target="tpu_custom_call", output_to_operand_aliasing={{0}: (1, {}), {1}: (3, {}), {2}: (4, {})} | custom-call | tf_op jit(solution)/shard_map/advance_3/pallas_call | solution.py:328
  54.0 1.2 collective-permute-start.12
  55.2 2.7 %advance_4.4 = (f32[4,64,8192]{2,1,0:T(8,128)S(1)}, f32[4,64,8192]{2,1,0:T(8,128)S(1)}, f32[8,8192]{1,0:T(8,128)S(1)}, f32[3,64,128]{2,1,0:T(8,128)S(1)}, f32[520,128]{1,0:T(8,128)S(1)}) custom-call(s32[1]{0:T(128)} %bitcast.refs_0_, f32[4,64,8192]{2,1,0:T(8,128)S(1)} %get-tuple-element.147.refs_1_, ...), custom_call_target="tpu_custom_call", output_to_operand_aliasing={{0}: (1, {}), {1}: (3, {}), {2}: (4, {})} | custom-call | tf_op jit(solution)/shard_map/advance_4/pallas_call | solution.py:328
  58.0 1.0 collective-permute-start.14
  58.9 2.7 %advance_5.4 = (f32[4,64,8192]{2,1,0:T(8,128)S(1)}, f32[4,64,8192]{2,1,0:T(8,128)S(1)}, f32[8,8192]{1,0:T(8,128)S(1)}, f32[3,64,128]{2,1,0:T(8,128)S(1)}, f32[520,128]{1,0:T(8,128)S(1)}) custom-call(s32[1]{0:T(128)} %bitcast.refs_0_, f32[4,64,8192]{2,1,0:T(8,128)S(1)} %get-tuple-element.153.refs_1_, ...), custom_call_target="tpu_custom_call", output_to_operand_aliasing={{0}: (1, {}), {1}: (3, {}), {2}: (4, {})} | custom-call | tf_op jit(solution)/shard_map/advance_5/pallas_call | solution.py:328
  61.6 1.2 collective-permute-start.15
  62.8 1.9 %collective-permute-done.11.refs_8_ = f32[3,64,128]{2,1,0:T(8,128)S(1)} collective-permute-done((f32[3,64,128]{2,1,0:T(8,128)S(1)}, f32[3,64,128]{2,1,0:T(8,128)S(1)}, u32[]{:S(2)}, u32[]{:S(2)}) %collective-permute-start.11) | collective-permute-done | bytes 98336 | tf_op jit(solution)/shard_map/ppermute | solution.py:356
  64.7 1.9 %collective-permute-start.13 = (f32[3,64,128]{2,1,0:T(8,128)S(1)}, f32[3,64,128]{2,1,0:T(8,128)S(1)}, u32[]{:S(2)}, u32[]{:S(2)}) collective-permute-start(f32[3,64,128]{2,1,0:T(8,128)S(1)} %get-tuple-element.171), channel_id=1, source_target_pairs={{1,0},{2,1},{3,2},{4,3},{5,4},{6,5},{7,6},{8,7},{9,8},{10,9},{11,1... | collective-permute-start | bytes 294920 | tf_op jit(solution)/shard_map/ppermute | solution.py:359
  66.6 2.6 %advance_0.4 = (f32[4,64,8192]{2,1,0:T(8,128)S(1)}, f32[8,8192]{1,0:T(8,128)S(1)}, f32[520,128]{1,0:T(8,128)S(1)}) custom-call(s32[1]{0:T(128)} %bitcast.refs_0_, f32[4,64,8192]{2,1,0:T(8,128)S(1)} %get-tuple-element.159.refs_1_, f32[8,8192]{1,0:T(8,128)S(1)} %get-tuple-element.137.refs_2_, ...), custom_call_target="tpu_custom_call", output_to_operand_aliasing={{0}: (3, {}), {1}: (4, {})} | custom-call | tf_op jit(solution)/shard_map/advance_0/pallas_call | solution.py:328
  69.3 0.9 collective-permute-start.16
  70.2 2.6 %advance_7.4 = (f32[4,64,8192]{2,1,0:T(8,128)S(1)}, f32[8,8192]{1,0:T(8,128)S(1)}, f32[520,128]{1,0:T(8,128)S(1)}) custom-call(s32[1]{0:T(128)} %bitcast.refs_0_, f32[4,64,8192]{2,1,0:T(8,128)S(1)} %get-tuple-element.159.refs_1_, f32[8,8192]{1,0:T(8,128)S(1)} %get-tuple-element.137.refs_2_, ...), custom_call_target="tpu_custom_call", output_to_operand_aliasing={{0}: (3, {}), {1}: (4, {})} | custom-call | tf_op jit(solution)/shard_map/advance_7/pallas_call | solution.py:328
  72.9 1.2 collective-permute-start.17
  74.1 2.6 %advance_6.4 = (f32[4,64,8192]{2,1,0:T(8,128)S(1)}, f32[8,8192]{1,0:T(8,128)S(1)}, f32[520,128]{1,0:T(8,128)S(1)}) custom-call(s32[1]{0:T(128)} %bitcast.refs_0_, f32[4,64,8192]{2,1,0:T(8,128)S(1)} %get-tuple-element.159.refs_1_, f32[8,8192]{1,0:T(8,128)S(1)} %get-tuple-element.137.refs_2_, ...), custom_call_target="tpu_custom_call", output_to_operand_aliasing={{0}: (3, {}), {1}: (4, {})} | custom-call | tf_op jit(solution)/shard_map/advance_6/pallas_call | solution.py:328
  76.7 0.9 collective-permute-start.18
  77.7 1.8 %collective-permute-done.15.refs_5_ = f32[520,128]{1,0:T(8,128)S(1)} collective-permute-done((f32[520,128]{1,0:T(8,128)S(1)}, f32[520,128]{1,0:T(8,128)S(1)}, u32[]{:S(2)}, u32[]{:S(2)}) %collective-permute-start.15) | collective-permute-done | bytes 266272 | tf_op jit(solution)/shard_map/ppermute | solution.py:353
  79.5 2.6 %advance_1.4 = (f32[4,64,8192]{2,1,0:T(8,128)S(1)}, f32[8,8192]{1,0:T(8,128)S(1)}, f32[520,128]{1,0:T(8,128)S(1)}) custom-call(s32[1]{0:T(128)} %bitcast.refs_0_, f32[4,64,8192]{2,1,0:T(8,128)S(1)} %get-tuple-element.159.refs_1_, f32[8,8192]{1,0:T(8,128)S(1)} %get-tuple-element.137.refs_2_, ...), custom_call_target="tpu_custom_call", output_to_operand_aliasing={{0}: (3, {}), {1}: (4, {})} | custom-call | tf_op jit(solution)/shard_map/advance_1/pallas_call | solution.py:328
  82.1 0.5 collective-permute-start.20
  82.6 2.6 %collective-permute-done.16.refs_3_ = f32[520,128]{1,0:T(8,128)S(1)} collective-permute-done((f32[520,128]{1,0:T(8,128)S(1)}, f32[520,128]{1,0:T(8,128)S(1)}, u32[]{:S(2)}, u32[]{:S(2)}) %collective-permute-start.16) | collective-permute-done | bytes 266272 | tf_op jit(solution)/shard_map/ppermute | solution.py:353
  85.2 2.7 %advance_3.5 = (f32[4,64,8192]{2,1,0:T(8,128)S(1)}, f32[4,64,8192]{2,1,0:T(8,128)S(1)}, f32[8,8192]{1,0:T(8,128)S(1)}, f32[3,64,128]{2,1,0:T(8,128)S(1)}, f32[520,128]{1,0:T(8,128)S(1)}) custom-call(s32[1]{0:T(128)} %bitcast.refs_0_, f32[4,64,8192]{2,1,0:T(8,128)S(1)} %get-tuple-element.182.refs_1_, ...), custom_call_target="tpu_custom_call", output_to_operand_aliasing={{0}: (1, {})} | custom-call | tf_op jit(solution)/shard_map/advance_3/pallas_call | solution.py:328
  87.9 3.7 %collective-permute-start.19 = (f32[3,64,128]{2,1,0:T(8,128)S(1)}, f32[3,64,128]{2,1,0:T(8,128)S(1)}, u32[]{:S(2)}, u32[]{:S(2)}) collective-permute-start(f32[3,64,128]{2,1,0:T(8,128)S(1)} %get-tuple-element.193), channel_id=1, source_target_pairs={{1,0},{2,1},{3,2},{4,3},{5,4},{6,5},{7,6},{8,7},{9,8},{10,9},{11,1... | collective-permute-start | bytes 294920 | tf_op jit(solution)/shard_map/ppermute | solution.py:359
  91.5 2.7 %advance_4.5 = (f32[4,64,8192]{2,1,0:T(8,128)S(1)}, f32[4,64,8192]{2,1,0:T(8,128)S(1)}, f32[8,8192]{1,0:T(8,128)S(1)}, f32[3,64,128]{2,1,0:T(8,128)S(1)}, f32[520,128]{1,0:T(8,128)S(1)}) custom-call(s32[1]{0:T(128)} %bitcast.refs_0_, f32[4,64,8192]{2,1,0:T(8,128)S(1)} %get-tuple-element.185.refs_1_, ...), custom_call_target="tpu_custom_call", output_to_operand_aliasing={{0}: (1, {}), {1}: (3, {}), {2}: (4, {})} | custom-call | tf_op jit(solution)/shard_map/advance_4/pallas_call | solution.py:328
  94.5 2.1 %collective-permute-done.18.refs_5_ = f32[520,128]{1,0:T(8,128)S(1)} collective-permute-done((f32[520,128]{1,0:T(8,128)S(1)}, f32[520,128]{1,0:T(8,128)S(1)}, u32[]{:S(2)}, u32[]{:S(2)}) %collective-permute-start.18) | collective-permute-done | bytes 266272 | tf_op jit(solution)/shard_map/ppermute | solution.py:353
  97.0 2.7 %advance_7.5 = (f32[4,64,8192]{2,1,0:T(8,128)S(1)}, f32[4,64,8192]{2,1,0:T(8,128)S(1)}, f32[8,8192]{1,0:T(8,128)S(1)}, f32[520,128]{1,0:T(8,128)S(1)}) custom-call(s32[1]{0:T(128)} %bitcast.refs_0_, f32[4,64,8192]{2,1,0:T(8,128)S(1)} %get-tuple-element.189.refs_1_, ...), custom_call_target="tpu_custom_call", output_to_operand_aliasing={{0}: (1, {}), {1}: (3, {}), {2}: (4, {})} | custom-call | tf_op jit(solution)/shard_map/advance_7/pallas_call | solution.py:328
  99.7 1.7 %collective-permute-start.24 = (f32[520,128]{1,0:T(8,128)S(1)}, f32[520,128]{1,0:T(8,128)S(1)}, u32[]{:S(2)}, u32[]{:S(2)}) collective-permute-start(f32[520,128]{1,0:T(8,128)S(1)} %get-tuple-element.209), channel_id=1, source_target_pairs={{0,16},{16,0},{1,17},{17,1},{2,18},{18,2},{3,19},{19,3},{4,20},{20... | collective-permute-start | bytes 798728 | tf_op jit(solution)/shard_map/ppermute | solution.py:353
  101.4 0.9 collective-permute-done.20.refs_5_
  102.3 2.7 %advance_0.5 = (f32[4,64,8192]{2,1,0:T(8,128)S(1)}, f32[4,64,8192]{2,1,0:T(8,128)S(1)}, f32[8,8192]{1,0:T(8,128)S(1)}, f32[520,128]{1,0:T(8,128)S(1)}) custom-call(s32[1]{0:T(128)} %bitcast.refs_0_, f32[4,64,8192]{2,1,0:T(8,128)S(1)} %get-tuple-element.194.refs_1_, ...), custom_call_target="tpu_custom_call", output_to_operand_aliasing={{0}: (1, {}), {1}: (3, {}), {2}: (4, {})} | custom-call | tf_op jit(solution)/shard_map/advance_0/pallas_call | solution.py:328
  105.5 2.5 %collective-permute-done.22.refs_5_ = f32[520,128]{1,0:T(8,128)S(1)} collective-permute-done((f32[520,128]{1,0:T(8,128)S(1)}, f32[520,128]{1,0:T(8,128)S(1)}, u32[]{:S(2)}, u32[]{:S(2)}) %collective-permute-start.22) | collective-permute-done | bytes 266272 | tf_op jit(solution)/shard_map/ppermute | solution.py:353
  108.0 2.6 %advance_5.5 = (f32[4,64,8192]{2,1,0:T(8,128)S(1)}, f32[8,8192]{1,0:T(8,128)S(1)}, f32[4,64,8192]{2,1,0:T(8,128)}, f32[520,128]{1,0:T(8,128)S(1)}) custom-call(s32[1]{0:T(128)} %bitcast.refs_0_, f32[4,64,8192]{2,1,0:T(8,128)S(1)} %get-tuple-element.199.refs_1_, ...), custom_call_target="tpu_custom_call", output_to_operand_aliasing={{0}: (3, {}), {1}: (4, {})} | custom-call | tf_op jit(solution)/shard_map/advance_5/pallas_call | solution.py:328
  110.6 3.1 %collective-permute-done.23.refs_5_ = f32[520,128]{1,0:T(8,128)S(1)} collective-permute-done((f32[520,128]{1,0:T(8,128)S(1)}, f32[520,128]{1,0:T(8,128)S(1)}, u32[]{:S(2)}, u32[]{:S(2)}) %collective-permute-start.23) | collective-permute-done | bytes 266272 | tf_op jit(solution)/shard_map/ppermute | solution.py:353
  113.7 2.6 %advance_6.5 = (f32[4,64,8192]{2,1,0:T(8,128)S(1)}, f32[8,8192]{1,0:T(8,128)S(1)}, f32[4,64,8192]{2,1,0:T(8,128)}, f32[520,128]{1,0:T(8,128)S(1)}) custom-call(s32[1]{0:T(128)} %bitcast.refs_0_, f32[4,64,8192]{2,1,0:T(8,128)S(1)} %get-tuple-element.199.refs_1_, ...), custom_call_target="tpu_custom_call", output_to_operand_aliasing={{0}: (3, {}), {1}: (4, {}), {2}: (6, {})} | custom-call | tf_op jit(solution)/shard_map/advance_6/pallas_call | solution.py:328
  116.8 1.6 %collective-permute-start.26 = (f32[520,128]{1,0:T(8,128)S(1)}, f32[520,128]{1,0:T(8,128)S(1)}, u32[]{:S(2)}, u32[]{:S(2)}) collective-permute-start(f32[520,128]{1,0:T(8,128)S(1)} %get-tuple-element.217), channel_id=1, source_target_pairs={{0,16},{16,0},{1,17},{17,1},{2,18},{18,2},{3,19},{19,3},{4,20},{20... | collective-permute-start | bytes 798728 | tf_op jit(solution)/shard_map/ppermute | solution.py:353
  118.4 1.0 collective-permute-done.24.refs_5_
  119.4 2.6 %advance_1.5 = (f32[4,64,8192]{2,1,0:T(8,128)S(1)}, f32[8,8192]{1,0:T(8,128)S(1)}, f32[4,64,8192]{2,1,0:T(8,128)}, f32[520,128]{1,0:T(8,128)S(1)}) custom-call(s32[1]{0:T(128)} %bitcast.refs_0_, f32[4,64,8192]{2,1,0:T(8,128)S(1)} %get-tuple-element.199.refs_1_, ...), custom_call_target="tpu_custom_call", output_to_operand_aliasing={{0}: (3, {}), {1}: (4, {}), {2}: (6, {})} | custom-call | tf_op jit(solution)/shard_map/advance_1/pallas_call | solution.py:328
  122.0 0.5 collective-permute-start.28
  122.5 2.6 %collective-permute-done.25.refs_5_ = f32[520,128]{1,0:T(8,128)S(1)} collective-permute-done((f32[520,128]{1,0:T(8,128)S(1)}, f32[520,128]{1,0:T(8,128)S(1)}, u32[]{:S(2)}, u32[]{:S(2)}) %collective-permute-start.25) | collective-permute-done | bytes 266272 | tf_op jit(solution)/shard_map/ppermute | solution.py:353
  125.1 2.6 %advance_2.5 = (f32[4,64,8192]{2,1,0:T(8,128)S(1)}, f32[8,8192]{1,0:T(8,128)S(1)}, f32[4,64,8192]{2,1,0:T(8,128)}, f32[520,128]{1,0:T(8,128)S(1)}) custom-call(s32[1]{0:T(128)} %bitcast.refs_0_, f32[4,64,8192]{2,1,0:T(8,128)S(1)} %get-tuple-element.199.refs_1_, ...), custom_call_target="tpu_custom_call", output_to_operand_aliasing={{0}: (3, {}), {1}: (4, {}), {2}: (6, {})} | custom-call | tf_op jit(solution)/shard_map/advance_2/pallas_call | solution.py:328
  128.2 8.3 %collective-permute-done.26.refs_3_ = f32[520,128]{1,0:T(8,128)S(1)} collective-permute-done((f32[520,128]{1,0:T(8,128)S(1)}, f32[520,128]{1,0:T(8,128)S(1)}, u32[]{:S(2)}, u32[]{:S(2)}) %collective-permute-start.26) | collective-permute-done | bytes 266272 | tf_op jit(solution)/shard_map/ppermute | solution.py:353
  136.5 1.0 complete.4
  137.6 1.0 complete.5
  138.6 3.6 %collective-permute-done.28.refs_3_ = f32[520,128]{1,0:T(8,128)S(1)} collective-permute-done((f32[520,128]{1,0:T(8,128)S(1)}, f32[520,128]{1,0:T(8,128)S(1)}, u32[]{:S(2)}, u32[]{:S(2)}) %collective-permute-start.28) | collective-permute-done | bytes 266272 | tf_op jit(solution)/shard_map/ppermute | solution.py:353
  142.2 1.0 complete.6
  143.3 3.0 %collective-permute-done.29.refs_3_ = f32[520,128]{1,0:T(8,128)S(1)} collective-permute-done((f32[520,128]{1,0:T(8,128)S(1)}, f32[520,128]{1,0:T(8,128)S(1)}, u32[]{:S(2)}, u32[]{:S(2)}) %collective-permute-start.29) | collective-permute-done | bytes 266272 | tf_op jit(solution)/shard_map/ppermute | solution.py:353
  146.2 1.0 complete.7
  (33 shorter events, 2.3 us)
Async XLA Ops:
  3.8 23.3 %collective-permute-start = (f32[520,128]{1,0:T(8,128)S(1)}, f32[520,128]{1,0:T(8,128)S(1)}, u32[]{:S(2)}, u32[]{:S(2)}) collective-permute-start(f32[520,128]{1,0:T(8,128)S(1)} %get-tuple-element.126), channel_id=1, source_target_pairs={{0,16},{16,0},{1,17},{17,1},{2,18},{18,2},{3,19},{19,3},{4,20},{20... | collective-permute-start | bytes 798728 | tf_op jit(solution)/shard_map/ppermute | solution.py:353
  10.4 2.0 %copy-start.2 = (bf16[4,4,512,256]{3,2,1,0:T(8,128)(2,1)}, bf16[4,4,512,256]{3,2,1,0:T(8,128)(2,1)S(1)}, u32[]{:S(2)}) copy-start(bf16[4,4,512,256]{3,2,1,0:T(8,128)(2,1)S(1)} %get-tuple-element.139.refs_4_.refs_7_) | copy-start | bytes 12582916
  12.4 18.2 %collective-permute-start.1 = (f32[520,128]{1,0:T(8,128)S(1)}, f32[520,128]{1,0:T(8,128)S(1)}, u32[]{:S(2)}, u32[]{:S(2)}) collective-permute-start(f32[520,128]{1,0:T(8,128)S(1)} %get-tuple-element.129), channel_id=1, source_target_pairs={{0,16},{16,0},{1,17},{17,1},{2,18},{18,2},{3,19},{19,3},{4,20},{20... | collective-permute-start | bytes 798728 | tf_op jit(solution)/shard_map/ppermute | solution.py:353
  15.9 5.6 %copy-start = (bf16[4,4,512,256]{3,2,1,0:T(8,128)(2,1)}, bf16[4,4,512,256]{3,2,1,0:T(8,128)(2,1)S(1)}, u32[]{:S(2)}) copy-start(bf16[4,4,512,256]{3,2,1,0:T(8,128)(2,1)S(1)} %get-tuple-element.145.refs_6_.refs_4_) | copy-start | bytes 12582916
  15.9 20.4 %collective-permute-start.2 = (f32[520,128]{1,0:T(8,128)S(1)}, f32[520,128]{1,0:T(8,128)S(1)}, u32[]{:S(2)}, u32[]{:S(2)}) collective-permute-start(f32[520,128]{1,0:T(8,128)S(1)} %get-tuple-element.132), channel_id=1, source_target_pairs={{0,16},{16,0},{1,17},{17,1},{2,18},{18,2},{3,19},{19,3},{4,20},{20... | collective-permute-start | bytes 798728 | tf_op jit(solution)/shard_map/ppermute | solution.py:353
  21.6 18.9 %collective-permute-start.5 = (f32[520,128]{1,0:T(8,128)S(1)}, f32[520,128]{1,0:T(8,128)S(1)}, u32[]{:S(2)}, u32[]{:S(2)}) collective-permute-start(f32[520,128]{1,0:T(8,128)S(1)} %get-tuple-element.135), channel_id=1, source_target_pairs={{0,16},{16,0},{1,17},{17,1},{2,18},{18,2},{3,19},{19,3},{4,20},{20... | collective-permute-start | bytes 798728 | tf_op jit(solution)/shard_map/ppermute | solution.py:353
  23.7 11.1 %collective-permute-start.4 = (f32[3,64,128]{2,1,0:T(8,128)S(1)}, f32[3,64,128]{2,1,0:T(8,128)S(1)}, u32[]{:S(2)}, u32[]{:S(2)}) collective-permute-start(f32[3,64,128]{2,1,0:T(8,128)S(1)} %get-tuple-element.229), channel_id=1, source_target_pairs={{1,0},{2,1},{3,2},{4,3},{5,4},{6,5},{7,6},{8,7},{9,8},{10,9},{11,1... | collective-permute-start | bytes 294920 | tf_op jit(solution)/shard_map/ppermute | solution.py:359
  27.1 9.3 %collective-permute-start.3 = (f32[3,64,128]{2,1,0:T(8,128)S(1)}, f32[3,64,128]{2,1,0:T(8,128)S(1)}, u32[]{:S(2)}, u32[]{:S(2)}) collective-permute-start(f32[3,64,128]{2,1,0:T(8,128)S(1)} %get-tuple-element.230), channel_id=1, source_target_pairs={{0,1},{1,2},{2,3},{3,4},{4,5},{5,6},{6,7},{7,8},{8,9},{9,10},{10,1... | collective-permute-start | bytes 294920 | tf_op jit(solution)/shard_map/ppermute | solution.py:356
  30.6 14.9 %collective-permute-start.6 = (f32[520,128]{1,0:T(8,128)S(1)}, f32[520,128]{1,0:T(8,128)S(1)}, u32[]{:S(2)}, u32[]{:S(2)}) collective-permute-start(f32[520,128]{1,0:T(8,128)S(1)} %get-tuple-element.138), channel_id=1, source_target_pairs={{0,16},{16,0},{1,17},{17,1},{2,18},{18,2},{3,19},{19,3},{4,20},{20... | collective-permute-start | bytes 798728 | tf_op jit(solution)/shard_map/ppermute | solution.py:353
  34.8 16.5 %collective-permute-start.7 = (f32[520,128]{1,0:T(8,128)S(1)}, f32[520,128]{1,0:T(8,128)S(1)}, u32[]{:S(2)}, u32[]{:S(2)}) collective-permute-start(f32[520,128]{1,0:T(8,128)S(1)} %get-tuple-element.144), channel_id=1, source_target_pairs={{0,16},{16,0},{1,17},{17,1},{2,18},{18,2},{3,19},{19,3},{4,20},{20... | collective-permute-start | bytes 798728 | tf_op jit(solution)/shard_map/ppermute | solution.py:353
  39.8 15.3 %collective-permute-start.8 = (f32[520,128]{1,0:T(8,128)S(1)}, f32[520,128]{1,0:T(8,128)S(1)}, u32[]{:S(2)}, u32[]{:S(2)}) collective-permute-start(f32[520,128]{1,0:T(8,128)S(1)} %get-tuple-element.150), channel_id=1, source_target_pairs={{0,16},{16,0},{1,17},{17,1},{2,18},{18,2},{3,19},{19,3},{4,20},{20... | collective-permute-start | bytes 798728 | tf_op jit(solution)/shard_map/ppermute | solution.py:353
  44.0 7.3 %copy-start.1 = (bf16[4,4,512,256]{3,2,1,0:T(8,128)(2,1)S(1)}, bf16[4,4,512,256]{3,2,1,0:T(8,128)(2,1)}, u32[]{:S(2)}) copy-start(bf16[4,4,512,256]{3,2,1,0:T(8,128)(2,1)} %copy-done) | copy-start | bytes 12582916
  44.0 14.9 %collective-permute-start.9 = (f32[520,128]{1,0:T(8,128)S(1)}, f32[520,128]{1,0:T(8,128)S(1)}, u32[]{:S(2)}, u32[]{:S(2)}) collective-permute-start(f32[520,128]{1,0:T(8,128)S(1)} %get-tuple-element.156), channel_id=1, source_target_pairs={{0,16},{16,0},{1,17},{17,1},{2,18},{18,2},{3,19},{19,3},{4,20},{20... | collective-permute-start | bytes 798728 | tf_op jit(solution)/shard_map/ppermute | solution.py:353
  45.6 2.2 %copy-start.3 = (bf16[4,4,512,256]{3,2,1,0:T(8,128)(2,1)S(1)}, bf16[4,4,512,256]{3,2,1,0:T(8,128)(2,1)}, u32[]{:S(2)}) copy-start(bf16[4,4,512,256]{3,2,1,0:T(8,128)(2,1)} %copy-done.2) | copy-start | bytes 12582916
  50.4 16.3 %collective-permute-start.10 = (f32[520,128]{1,0:T(8,128)S(1)}, f32[520,128]{1,0:T(8,128)S(1)}, u32[]{:S(2)}, u32[]{:S(2)}) collective-permute-start(f32[520,128]{1,0:T(8,128)S(1)} %get-tuple-element.162), channel_id=1, source_target_pairs={{0,16},{16,0},{1,17},{17,1},{2,18},{18,2},{3,19},{19,3},{4,20},{20... | collective-permute-start | bytes 798728 | tf_op jit(solution)/shard_map/ppermute | solution.py:353
  54.0 16.3 %collective-permute-start.12 = (f32[520,128]{1,0:T(8,128)S(1)}, f32[520,128]{1,0:T(8,128)S(1)}, u32[]{:S(2)}, u32[]{:S(2)}) collective-permute-start(f32[520,128]{1,0:T(8,128)S(1)} %get-tuple-element.168), channel_id=1, source_target_pairs={{0,16},{16,0},{1,17},{17,1},{2,18},{18,2},{3,19},{19,3},{4,20},{20... | collective-permute-start | bytes 798728 | tf_op jit(solution)/shard_map/ppermute | solution.py:353
  57.9 6.8 %collective-permute-start.11 = (f32[3,64,128]{2,1,0:T(8,128)S(1)}, f32[3,64,128]{2,1,0:T(8,128)S(1)}, u32[]{:S(2)}, u32[]{:S(2)}) collective-permute-start(f32[3,64,128]{2,1,0:T(8,128)S(1)} %get-tuple-element.165), channel_id=1, source_target_pairs={{0,1},{1,2},{2,3},{3,4},{4,5},{5,6},{6,7},{7,8},{8,9},{9,10},{10,1... | collective-permute-start | bytes 294920 | tf_op jit(solution)/shard_map/ppermute | solution.py:356
  58.0 16.1 %collective-permute-start.14 = (f32[520,128]{1,0:T(8,128)S(1)}, f32[520,128]{1,0:T(8,128)S(1)}, u32[]{:S(2)}, u32[]{:S(2)}) collective-permute-start(f32[520,128]{1,0:T(8,128)S(1)} %get-tuple-element.174), channel_id=1, source_target_pairs={{0,16},{16,0},{1,17},{17,1},{2,18},{18,2},{3,19},{19,3},{4,20},{20... | collective-permute-start | bytes 798728 | tf_op jit(solution)/shard_map/ppermute | solution.py:353
  61.6 17.8 %collective-permute-start.15 = (f32[520,128]{1,0:T(8,128)S(1)}, f32[520,128]{1,0:T(8,128)S(1)}, u32[]{:S(2)}, u32[]{:S(2)}) collective-permute-start(f32[520,128]{1,0:T(8,128)S(1)} %get-tuple-element.179), channel_id=1, source_target_pairs={{0,16},{16,0},{1,17},{17,1},{2,18},{18,2},{3,19},{19,3},{4,20},{20... | collective-permute-start | bytes 798728 | tf_op jit(solution)/shard_map/ppermute | solution.py:353
  64.7 5.5 %collective-permute-start.13 = (f32[3,64,128]{2,1,0:T(8,128)S(1)}, f32[3,64,128]{2,1,0:T(8,128)S(1)}, u32[]{:S(2)}, u32[]{:S(2)}) collective-permute-start(f32[3,64,128]{2,1,0:T(8,128)S(1)} %get-tuple-element.171), channel_id=1, source_target_pairs={{1,0},{2,1},{3,2},{4,3},{5,4},{6,5},{7,6},{8,7},{9,8},{10,9},{11,1... | collective-permute-start | bytes 294920 | tf_op jit(solution)/shard_map/ppermute | solution.py:359
  69.3 15.9 %collective-permute-start.16 = (f32[520,128]{1,0:T(8,128)S(1)}, f32[520,128]{1,0:T(8,128)S(1)}, u32[]{:S(2)}, u32[]{:S(2)}) collective-permute-start(f32[520,128]{1,0:T(8,128)S(1)} %get-tuple-element.184), channel_id=1, source_target_pairs={{0,16},{16,0},{1,17},{17,1},{2,18},{18,2},{3,19},{19,3},{4,20},{20... | collective-permute-start | bytes 798728 | tf_op jit(solution)/shard_map/ppermute | solution.py:353
  72.9 18.7 %collective-permute-start.17 = (f32[520,128]{1,0:T(8,128)S(1)}, f32[520,128]{1,0:T(8,128)S(1)}, u32[]{:S(2)}, u32[]{:S(2)}) collective-permute-start(f32[520,128]{1,0:T(8,128)S(1)} %get-tuple-element.188), channel_id=1, source_target_pairs={{0,16},{16,0},{1,17},{17,1},{2,18},{18,2},{3,19},{19,3},{4,20},{20... | collective-permute-start | bytes 798728 | tf_op jit(solution)/shard_map/ppermute | solution.py:353
  76.7 19.8 %collective-permute-start.18 = (f32[520,128]{1,0:T(8,128)S(1)}, f32[520,128]{1,0:T(8,128)S(1)}, u32[]{:S(2)}, u32[]{:S(2)}) collective-permute-start(f32[520,128]{1,0:T(8,128)S(1)} %get-tuple-element.192), channel_id=1, source_target_pairs={{0,16},{16,0},{1,17},{17,1},{2,18},{18,2},{3,19},{19,3},{4,20},{20... | collective-permute-start | bytes 798728 | tf_op jit(solution)/shard_map/ppermute | solution.py:353
  82.1 20.2 %collective-permute-start.20 = (f32[520,128]{1,0:T(8,128)S(1)}, f32[520,128]{1,0:T(8,128)S(1)}, u32[]{:S(2)}, u32[]{:S(2)}) collective-permute-start(f32[520,128]{1,0:T(8,128)S(1)} %get-tuple-element.197), channel_id=1, source_target_pairs={{0,16},{16,0},{1,17},{17,1},{2,18},{18,2},{3,19},{19,3},{4,20},{20... | collective-permute-start | bytes 798728 | tf_op jit(solution)/shard_map/ppermute | solution.py:353
  87.9 9.1 %collective-permute-start.19 = (f32[3,64,128]{2,1,0:T(8,128)S(1)}, f32[3,64,128]{2,1,0:T(8,128)S(1)}, u32[]{:S(2)}, u32[]{:S(2)}) collective-permute-start(f32[3,64,128]{2,1,0:T(8,128)S(1)} %get-tuple-element.193), channel_id=1, source_target_pairs={{1,0},{2,1},{3,2},{4,3},{5,4},{6,5},{7,6},{8,7},{9,8},{10,9},{11,1... | collective-permute-start | bytes 294920 | tf_op jit(solution)/shard_map/ppermute | solution.py:359
  94.2 8.0 %collective-permute-start.21 = (f32[3,64,128]{2,1,0:T(8,128)S(1)}, f32[3,64,128]{2,1,0:T(8,128)S(1)}, u32[]{:S(2)}, u32[]{:S(2)}) collective-permute-start(f32[3,64,128]{2,1,0:T(8,128)S(1)} %get-tuple-element.198), channel_id=1, source_target_pairs={{0,1},{1,2},{2,3},{3,4},{4,5},{5,6},{6,7},{7,8},{8,9},{9,10},{10,1... | collective-permute-start | bytes 294920 | tf_op jit(solution)/shard_map/ppermute | solution.py:356
  94.3 13.7 %collective-permute-start.22 = (f32[520,128]{1,0:T(8,128)S(1)}, f32[520,128]{1,0:T(8,128)S(1)}, u32[]{:S(2)}, u32[]{:S(2)}) collective-permute-start(f32[520,128]{1,0:T(8,128)S(1)} %get-tuple-element.202), channel_id=1, source_target_pairs={{0,16},{16,0},{1,17},{17,1},{2,18},{18,2},{3,19},{19,3},{4,20},{20... | collective-permute-start | bytes 798728 | tf_op jit(solution)/shard_map/ppermute | solution.py:353
  96.6 17.1 %collective-permute-start.23 = (f32[520,128]{1,0:T(8,128)S(1)}, f32[520,128]{1,0:T(8,128)S(1)}, u32[]{:S(2)}, u32[]{:S(2)}) collective-permute-start(f32[520,128]{1,0:T(8,128)S(1)} %get-tuple-element.205), channel_id=1, source_target_pairs={{0,16},{16,0},{1,17},{17,1},{2,18},{18,2},{3,19},{19,3},{4,20},{20... | collective-permute-start | bytes 798728 | tf_op jit(solution)/shard_map/ppermute | solution.py:353
  99.7 19.7 %collective-permute-start.24 = (f32[520,128]{1,0:T(8,128)S(1)}, f32[520,128]{1,0:T(8,128)S(1)}, u32[]{:S(2)}, u32[]{:S(2)}) collective-permute-start(f32[520,128]{1,0:T(8,128)S(1)} %get-tuple-element.209), channel_id=1, source_target_pairs={{0,16},{16,0},{1,17},{17,1},{2,18},{18,2},{3,19},{19,3},{4,20},{20... | collective-permute-start | bytes 798728 | tf_op jit(solution)/shard_map/ppermute | solution.py:353
  105.0 20.1 %collective-permute-start.25 = (f32[520,128]{1,0:T(8,128)S(1)}, f32[520,128]{1,0:T(8,128)S(1)}, u32[]{:S(2)}, u32[]{:S(2)}) collective-permute-start(f32[520,128]{1,0:T(8,128)S(1)} %get-tuple-element.213), channel_id=1, source_target_pairs={{0,16},{16,0},{1,17},{17,1},{2,18},{18,2},{3,19},{19,3},{4,20},{20... | collective-permute-start | bytes 798728 | tf_op jit(solution)/shard_map/ppermute | solution.py:353
  116.3 21.2 %collective-permute-start.27 = (f32[520,128]{1,0:T(8,128)S(1)}, f32[520,128]{1,0:T(8,128)S(1)}, u32[]{:S(2)}, u32[]{:S(2)}) collective-permute-start(f32[520,128]{1,0:T(8,128)S(1)} %get-tuple-element.220), channel_id=1, source_target_pairs={{0,16},{16,0},{1,17},{17,1},{2,18},{18,2},{3,19},{19,3},{4,20},{20... | collective-permute-start | bytes 798728 | tf_op jit(solution)/shard_map/ppermute | solution.py:353
  116.8 19.7 %collective-permute-start.26 = (f32[520,128]{1,0:T(8,128)S(1)}, f32[520,128]{1,0:T(8,128)S(1)}, u32[]{:S(2)}, u32[]{:S(2)}) collective-permute-start(f32[520,128]{1,0:T(8,128)S(1)} %get-tuple-element.217), channel_id=1, source_target_pairs={{0,16},{16,0},{1,17},{17,1},{2,18},{18,2},{3,19},{19,3},{4,20},{20... | collective-permute-start | bytes 798728 | tf_op jit(solution)/shard_map/ppermute | solution.py:353
  122.0 20.2 %collective-permute-start.28 = (f32[520,128]{1,0:T(8,128)S(1)}, f32[520,128]{1,0:T(8,128)S(1)}, u32[]{:S(2)}, u32[]{:S(2)}) collective-permute-start(f32[520,128]{1,0:T(8,128)S(1)} %get-tuple-element.223), channel_id=1, source_target_pairs={{0,16},{16,0},{1,17},{17,1},{2,18},{18,2},{3,19},{19,3},{4,20},{20... | collective-permute-start | bytes 798728 | tf_op jit(solution)/shard_map/ppermute | solution.py:353
  127.8 18.5 %collective-permute-start.29 = (f32[520,128]{1,0:T(8,128)S(1)}, f32[520,128]{1,0:T(8,128)S(1)}, u32[]{:S(2)}, u32[]{:S(2)}) collective-permute-start(f32[520,128]{1,0:T(8,128)S(1)} %get-tuple-element.226), channel_id=1, source_target_pairs={{0,16},{16,0},{1,17},{17,1},{2,18},{18,2},{3,19},{19,3},{4,20},{20... | collective-permute-start | bytes 798728 | tf_op jit(solution)/shard_map/ppermute | solution.py:353
where the time goes:
time: 148 us; the launch traced here: 147 us
  Pallas kernels  75.2 us (51%)
  starting transfers between devices  33.5 us (23%)
  waiting for transfers between devices  33.1 us (22%)
  local copies, waits for them, and re-layouts  5.16 us (3%)
    pallas_call x28, Pallas kernels, call(): pl.pallas_call(kernel, out_shape=[shape(name) for name in out_names], in_...  75.2 us
    ppermute x24, waiting for transfers between devices, shifted(): lax.ppermute(x, 'lev', [(i, (i + by) % groups) for i in range(groups)])  31.3 us
    ppermute x24, starting transfers between devices, shifted(): lax.ppermute(x, 'lev', [(i, (i + by) % groups) for i in range(groups)])  24.4 us
    ppermute x3, starting transfers between devices, from_high(): return lax.ppermute(x, 'tile', [((i + 1) % tiles, i) for i in range(tiles)])  8.97 us
    unnamed x8, local copies, waits for them, and re-layouts  4.2 us
  transfers between devices with their start and end apart: 30, of which 12 were waited for; matrix products, arithmetic and copies ran while one was open for 1% of the time, Pallas kernels for 48%

commit v1 on v0

--- a/solution.py
+++ b/solution.py
@@ -11,12 +11,15 @@
 LANES = 128
 BLOCK = 256
 SUBSTEPS = 3
-CHUNKS = 8
+SHARES = (4, 4, 4, 4, 4, 4, 4, 4)
+REBUILT = (1, 2)
+FIRST = 1
 LAG = 4
 EARLY = 6
+FIRST_END = 3
 UNROLL = 1
 EDGE_LAG = 2
-VMEM_LIMIT = 5 * 2**20
+VMEM_LIMIT = 6 * 2**20
 
 acoustic = 0.4
 half_acoustic = 0.5 * acoustic
@@ -49,17 +52,19 @@
         self.cells = cells
         self.directions = directions
         self.total = groups * levels
-        self.chunks = CHUNKS
-        self.width = cells // CHUNKS
+        self.chunks = len(SHARES)
+        self.widths = [cells * share // sum(SHARES) for share in SHARES]
+        self.starts = [sum(self.widths[:c]) for c in range(self.chunks)]
+        assert sum(self.widths) == cells and all(w % BLOCK == 0 for w in self.widths)
         self.extras = 1 if groups == 2 else 2
         self.rows = -(-(self.total + self.extras * groups) // 16) * 16
-        self.pieces = self.width // LANES
-        self.sent = (levels + self.extras) * self.pieces
+        self.pieces = [w // LANES for w in self.widths]
+        self.sent = [(levels + self.extras) * p for p in self.pieces]
         self.slots = self.schedule()
 
     def schedule(self):
         chunks = self.chunks
-        slots = [(0, (1 + q) % chunks) for q in range(chunks)]
+        slots = [(0, (FIRST + q) % chunks) for q in range(chunks)]
         for substep in range(1, SUBSTEPS):
             done = {c: t + LAG for t, (s, c) in enumerate(slots) if s == substep - 1}
             ready = {}
@@ -109,10 +114,10 @@
 
 
 def correct(plan, me, fields, x_ref, chunk, got):
-    levels, pieces = plan.levels, plan.pieces
+    levels, pieces = plan.levels, plan.pieces[chunk]
     row = lax.broadcasted_iota(jnp.int32, (levels, LANES), 0)
     for j in range(pieces):
-        cols = pl.ds(chunk * plan.width + j * LANES, LANES)
+        cols = pl.ds(plan.starts[chunk] + j * LANES, LANES)
         v = fields[3, :, cols]
         for g in got:
             v = v + g[j * levels : (j + 1) * levels, :]
@@ -166,8 +171,8 @@
             m_ref[i, r : r + tall, :] = x
 
 
-def advance(plan, pieces, src, origin, new, start, m, build, sum_ref, g_ref, f, x_ref, sends):
-    levels, width = plan.levels, plan.width
+def advance(plan, chunk, pieces, src, origin, new, start, m, build, sum_ref, g_ref, f, x_ref, sends):
+    levels, width = plan.levels, plan.widths[chunk]
     span = BLOCK + 2 * HALO
     blocks = width // BLOCK
     for ref, col, into, count in pieces:
@@ -179,16 +184,17 @@
 
     def block(b, carry):
         first = aligned(b * BLOCK, BLOCK)
+        here = b % m.shape[0] if isinstance(b, int) else b
         if build is not None and b > 0:
-            build(first, m.at[b])
+            build(first, m.at[here])
         cols = pl.ds(first, BLOCK)
         mine = pl.ds(aligned(origin + first, LANES), BLOCK)
         into = pl.ds(aligned(start + first, BLOCK), BLOCK)
         wide = pl.ds(first, span)
-        eh = dot(f[0 : 4 * levels, wide], m[b, 0])
-        el = dot(f[levels : 3 * levels, wide], m[b, 1])
-        nh = dot(f[4 * levels : 8 * levels, wide], m[b, 2])
-        nl = dot(f[5 * levels : 7 * levels, wide], m[b, 3])
+        eh = dot(f[0 : 4 * levels, wide], m[here, 0])
+        el = dot(f[levels : 3 * levels, wide], m[here, 1])
+        nh = dot(f[4 * levels : 8 * levels, wide], m[here, 2])
+        nl = dot(f[5 * levels : 7 * levels, wide], m[here, 3])
 
         def rows(x, i):
             return x[i * levels : (i + 1) * levels]
@@ -215,7 +221,7 @@
                 send[pl.ds(aligned(j * levels, 8), levels), :] = y[(s + 1) * levels : (s + 2) * levels, part]
                 for e in range(plan.extras):
                     at = plan.total + (s + 1) * plan.extras + e
-                    send[pl.ds(levels * plan.pieces + e * plan.pieces + j, 1), :] = y[at : at + 1, part]
+                    send[pl.ds((levels + e) * plan.pieces[chunk] + j, 1), :] = y[at : at + 1, part]
         return carry
 
     if build is None:
@@ -229,7 +235,8 @@
 
 
 def call(plan, arrays, outs, aliased, chunk=None, fixes=(), setup=False):
-    groups, levels, cells, width, chunks = plan.groups, plan.levels, plan.cells, plan.width, plan.chunks
+    groups, levels, cells, chunks = plan.groups, plan.levels, plan.cells, plan.chunks
+    start, width = (plan.starts[chunk], plan.widths[chunk]) if chunk is not None else (0, 0)
     in_names, out_names = list(arrays), list(outs)
     fresh = "prognostic" in arrays
 
@@ -238,8 +245,12 @@
         scratch["f"] = pltpu.VMEM((8 * levels, width + 2 * HALO), bf16)
     if fresh:
         scratch["win"] = pltpu.VMEM((4, levels, width + 2 * HALO), f32)
+    if "near" in arrays:
         scratch["near_v"] = pltpu.VMEM((plan.directions, width), jnp.int32)
         scratch["met_v"] = pltpu.VMEM((2, plan.directions, width), f32)
+        if "m" not in outs:
+            scratch["m"] = pltpu.VMEM((1, 4, BLOCK + 2 * HALO, BLOCK), bf16)
+            scratch["sums"] = pltpu.VMEM((8, width), f32)
     if setup:
         scratch["inv_v"] = pltpu.VMEM((plan.total, plan.total), f32)
     scratch["sems"] = pltpu.SemaphoreType.DMA((8,))
@@ -259,22 +270,23 @@
 
         who = r["me"][0]
         stores = []
+        loads = []
+        if "near" in r:
+            near = pl.ds(start, width)
+            loads = [copy(r["near"].at[:, near], r["near_v"]), copy(r["metric"].at[:, :, near], r["met_v"])]
         if fresh:
-            start = chunk * width
             lo = start if chunk == 0 else start - HALO
             hi = start + width if chunk == chunks - 1 else start + width + HALO
             into = lo - (start - HALO)
-            near = pl.ds(start, width)
-            loads = [copy(r["near"].at[:, near], r["near_v"]), copy(r["metric"].at[:, :, near], r["met_v"])]
             if setup:
                 loads.append(copy(r["inverse"], r["inv_v"]))
             late = copy(r["prognostic"].at[:, :, pl.ds(lo, hi - lo)], r["win"].at[:, :, pl.ds(into, hi - lo)])
-            for c in loads:
-                c.wait()
-            if setup:
-                operator(plan, who, r["inv_v"], r["g"])
+        for c in loads:
+            c.wait()
+        if setup:
+            operator(plan, who, r["inv_v"], r["g"])
         for name, b in fixes:
-            at = pl.ds(b * width, width)
+            at = pl.ds(plan.starts[b], plan.widths[b])
             got = [r[f"got_{name}{b}_{s}"] for s in range(groups - 1)]
             if "result" in r:
                 stores.append(copy(r[name].at[0:2, :, at], r["result"].at[0:2, :, at]))
@@ -286,7 +298,6 @@
             if b == chunks - 1 and "edge_high" in r:
                 r["edge_high"][...] = r[name][0:3, :, cells - HALO : cells]
         if chunk is not None:
-            start = chunk * width
             src, origin = (r["win"], HALO) if fresh else (r["old"], start)
             lo = origin if chunk == 0 else origin - HALO
             hi = origin + width if chunk == chunks - 1 else origin + width + HALO
@@ -297,16 +308,16 @@
                 pieces.append((r["halo_high"], 0, width + HALO, HALO))
             sends = [r[f"send{s}"] for s in range(groups - 1)]
             build = None
-            if fresh:
+            if "near" in r:
 
                 def build(first, m):
                     weights(plan, start, first, r["near_v"], r["met_v"], m, r["sums"])
 
+                build(0, r["m"].at[0])
             if fresh:
-                build(0, r["m"].at[0])
                 late.wait()
             advance(
-                plan, pieces, src, origin, r["new"], start, r["m"], build, r["sums"], r["g"], r["f"], r["new_x"], sends
+                plan, chunk, pieces, src, origin, r["new"], start, r["m"], build, r["sums"], r["g"], r["f"], r["new_x"], sends
             )
         for c in stores:
             c.wait()
@@ -402,11 +413,17 @@
         setup = g is None
         if chunk is not None:
             if substep == 0:
-                arrays.update(prognostic=prognostic, near=neighbours, metric=metric)
-                outs["m"] = shape((plan.width // BLOCK, 4, BLOCK + 2 * HALO, BLOCK), dtype=bf16)
-                outs["sums"] = shape((8, plan.width))
+                arrays["prognostic"] = prognostic
+                if chunk not in REBUILT:
+                    outs["m"] = shape((plan.widths[chunk] // BLOCK, 4, BLOCK + 2 * HALO, BLOCK), dtype=bf16)
+                    outs["sums"] = shape((8, plan.widths[chunk]))
+            if chunk in kept:
+                arrays.update(m=kept[chunk][0], sums=kept[chunk][1])
             else:
-                arrays.update(m=kept[chunk][0], sums=kept[chunk][1])
+                arrays.update(near=neighbours, metric=metric)
+            if slot == FIRST_END:
+                for i in range(groups - 1):
+                    arrays[f"first{i}"] = got[plan.slots[0]][i]
             early = slot == EARLY
             if chunk == 0 or early:
                 arrays["halo_low"] = halo_low
@@ -418,7 +435,7 @@
             else:
                 arrays["g"] = g
             for i in range(groups - 1):
-                outs[f"send{i}"] = shape((plan.sent, LANES))
+                outs[f"send{i}"] = shape((plan.sent[chunk], LANES))
         fixes = [(names[s], c) for s, c in due]
         res = call(plan, arrays, outs, aliased, chunk=chunk, fixes=fixes, setup=setup)
         g = res.get("g", g)
@@ -427,7 +444,7 @@
             if name in res:
                 state[s] = res[name], res.get(f"{name}_x", state[s][1] if s in state else None)
         if chunk is not None:
-            if substep == 0:
+            if "m" in res:
                 kept[chunk] = res["m"], res["sums"]
             got[substep, chunk] = [shifted(res[f"send{i}"], i + 1) for i in range(groups - 1)]
         if "edge_high" in res:

time: 148 us -> 147 us (level)
  starting transfers between devices: 33.5 us -> 45 us
  waiting for transfers between devices: 33.1 us -> 21.9 us
  local copies, waits for them, and re-layouts: 5.16 us -> 0.95 us
  Pallas kernels: 75.2 us -> 77.1 us
    ppermute x24, starting transfers between devices: 24.4 us -> 36.1 us  [shifted(): lax.ppermute(x, 'lev', [(i, (i + by) % groups) for i in range(groups)])]
    ppermute x24, waiting for transfers between devices: 31.3 us -> 20.7 us  [shifted(): lax.ppermute(x, 'lev', [(i, (i + by) % groups) for i in range(groups)])]
    unnamed x8 -> x0, local copies, waits for them, and re-layouts: 4.2 us -> none
    pallas_call x28, Pallas kernels: 75.2 us -> 77.1 us  [call(): pl.pallas_call(kernel, out_shape=[shape(name) for name in out_names], in_...]
  transfers between devices with their start and end apart: 30 -> 30, of which waited for: 12 -> 14; matrix products, arithmetic and copies ran while one was open for 1% -> 1% of each run, Pallas kernels for 48% -> 50%
where the time goes in v1:
time: 147 us; the launch traced here: 145 us
  Pallas kernels  77.1 us (52%)
  starting transfers between devices  45 us (31%)
  waiting for transfers between devices  21.9 us (15%)
    pallas_call x28, Pallas kernels, call(): pl.pallas_call(kernel, out_shape=[shape(name) for name in out_names], in_...  77.1 us
    ppermute x24, starting transfers between devices, shifted(): lax.ppermute(x, 'lev', [(i, (i + by) % groups) for i in range(groups)])  36.1 us
    ppermute x24, waiting for transfers between devices, shifted(): lax.ppermute(x, 'lev', [(i, (i + by) % groups) for i in range(groups)])  20.7 us
    ppermute x3, starting transfers between devices, from_high(): return lax.ppermute(x, 'tile', [((i + 1) % tiles, i) for i in range(tiles)])  8.83 us
  transfers between devices with their start and end apart: 30, of which 14 were waited for; matrix products, arithmetic and copies ran while one was open for 1% of the time, Pallas kernels for 50%

profile of v1, /device:TPU:0, one launch (start us, length us, event | category | flops | bytes accessed | tf_op | source)
XLA Modules:
  0.0 145.5 jit_solution(17343853778573537919)
XLA Ops:
  0.0 3.6 %advance_1.3 = (f32[4,64,8192]{2,1,0:T(8,128)S(1)}, f32[8,8192]{1,0:T(8,128)S(1)}, bf16[288,128]{1,0:T(8,128)(2,1)S(1)}, f32[520,128]{1,0:T(8,128)S(1)}) custom-call(s32[1]{0:T(128)} %bitcast.refs_0_, f32[4,64,8192]{2,1,0:T(8,128)} %refs_4_.14, s32[4,8192]{1,0:T(4,128)} %refs_7_.5, f32[2,4,8192]{2,1,0:T(4,128)} %refs_8_.3, f32[128,128]{1,0:T(8,128)} %bitcast.2), custom_call_target="tpu_custom_call" | custom-call | tf_op jit(solution)/shard_map/advance_1/pallas_call | solution.py:339
  3.6 3.0 %collective-permute-start = (f32[520,128]{1,0:T(8,128)S(1)}, f32[520,128]{1,0:T(8,128)S(1)}, u32[]{:S(2)}, u32[]{:S(2)}) collective-permute-start(f32[520,128]{1,0:T(8,128)S(1)} %get-tuple-element.120), channel_id=1, source_target_pairs={{0,16},{16,0},{1,17},{17,1},{2,18},{18,2},{3,19},{19,3},{4,20},{20... | collective-permute-start | bytes 798728 | tf_op jit(solution)/shard_map/ppermute | solution.py:364
  6.6 3.4 %advance_2.3 = (f32[4,64,8192]{2,1,0:T(8,128)S(1)}, f32[8,8192]{1,0:T(8,128)S(1)}, f32[520,128]{1,0:T(8,128)S(1)}) custom-call(s32[1]{0:T(128)} %bitcast.refs_0_, f32[4,64,8192]{2,1,0:T(8,128)S(1)} %get-tuple-element.113.refs_1_, f32[8,8192]{1,0:T(8,128)S(1)} %get-tuple-element.114.refs_2_, ...), custom_call_target="tpu_custom_call", output_to_operand_aliasing={{0}: (1, {}), {1}: (2, {})} | custom-call | tf_op jit(solution)/shard_map/advance_2/pallas_call | solution.py:339
  10.1 3.5 %advance_3.3 = (f32[4,64,8192]{2,1,0:T(8,128)S(1)}, f32[8,8192]{1,0:T(8,128)S(1)}, bf16[4,4,512,256]{3,2,1,0:T(8,128)(2,1)S(1)}, f32[8,1024]{1,0:T(8,128)S(1)}, f32[520,128]{1,0:T(8,128)S(1)}) custom-call(s32[1]{0:T(128)} %bitcast.refs_0_, f32[4,64,8192]{2,1,0:T(8,128)S(1)} %get-tuple-element.116.refs_1_, ...), custom_call_target="tpu_custom_call", output_to_operand_aliasing={{0}: (1, {}), {1}: (2, {})} | custom-call | tf_op jit(solution)/shard_map/advance_3/pallas_call | solution.py:339
  13.7 2.1 %collective-permute-start.2 = (f32[520,128]{1,0:T(8,128)S(1)}, f32[520,128]{1,0:T(8,128)S(1)}, u32[]{:S(2)}, u32[]{:S(2)}) collective-permute-start(f32[520,128]{1,0:T(8,128)S(1)} %get-tuple-element.128), channel_id=1, source_target_pairs={{0,16},{16,0},{1,17},{17,1},{2,18},{18,2},{3,19},{19,3},{4,20},{20... | collective-permute-start | bytes 798728 | tf_op jit(solution)/shard_map/ppermute | solution.py:364
  15.8 3.5 %advance_4.3 = (f32[4,64,8192]{2,1,0:T(8,128)S(1)}, f32[8,8192]{1,0:T(8,128)S(1)}, bf16[4,4,512,256]{3,2,1,0:T(8,128)(2,1)S(1)}, f32[8,1024]{1,0:T(8,128)S(1)}, f32[520,128]{1,0:T(8,128)S(1)}) custom-call(s32[1]{0:T(128)} %bitcast.refs_0_, f32[4,64,8192]{2,1,0:T(8,128)S(1)} %get-tuple-element.118.refs_1_, ...), custom_call_target="tpu_custom_call", output_to_operand_aliasing={{0}: (1, {}), {1}: (2, {})} | custom-call | tf_op jit(solution)/shard_map/advance_4/pallas_call | solution.py:339
  19.5 1.0 fusion
  20.5 3.2 %collective-permute-start.4 = (f32[3,64,128]{2,1,0:T(8,128)S(1)}, f32[3,64,128]{2,1,0:T(8,128)S(1)}, u32[]{:S(2)}, u32[]{:S(2)}) collective-permute-start(f32[3,64,128]{2,1,0:T(8,128)S(1)} %get-tuple-element.221), channel_id=1, source_target_pairs={{1,0},{2,1},{3,2},{4,3},{5,4},{6,5},{7,6},{8,7},{9,8},{10,9},{11,1... | collective-permute-start | bytes 294920 | tf_op jit(solution)/shard_map/ppermute | solution.py:370
  23.7 3.5 %advance_5.3 = (f32[4,64,8192]{2,1,0:T(8,128)S(1)}, f32[8,8192]{1,0:T(8,128)S(1)}, bf16[4,4,512,256]{3,2,1,0:T(8,128)(2,1)S(1)}, f32[8,1024]{1,0:T(8,128)S(1)}, f32[520,128]{1,0:T(8,128)S(1)}) custom-call(s32[1]{0:T(128)} %bitcast.refs_0_, f32[4,64,8192]{2,1,0:T(8,128)S(1)} %get-tuple-element.121.refs_1_, ...), custom_call_target="tpu_custom_call", output_to_operand_aliasing={{0}: (1, {}), {1}: (2, {})} | custom-call | tf_op jit(solution)/shard_map/advance_5/pallas_call | solution.py:339
  27.3 1.6 %collective-permute-start.6 = (f32[520,128]{1,0:T(8,128)S(1)}, f32[520,128]{1,0:T(8,128)S(1)}, u32[]{:S(2)}, u32[]{:S(2)}) collective-permute-start(f32[520,128]{1,0:T(8,128)S(1)} %get-tuple-element.134), channel_id=1, source_target_pairs={{0,16},{16,0},{1,17},{17,1},{2,18},{18,2},{3,19},{19,3},{4,20},{20... | collective-permute-start | bytes 798728 | tf_op jit(solution)/shard_map/ppermute | solution.py:364
  28.9 3.5 %advance_6.3 = (f32[4,64,8192]{2,1,0:T(8,128)S(1)}, f32[8,8192]{1,0:T(8,128)S(1)}, bf16[4,4,512,256]{3,2,1,0:T(8,128)(2,1)S(1)}, f32[8,1024]{1,0:T(8,128)S(1)}, f32[520,128]{1,0:T(8,128)S(1)}) custom-call(s32[1]{0:T(128)} %bitcast.refs_0_, f32[4,64,8192]{2,1,0:T(8,128)S(1)} %get-tuple-element.123.refs_1_, ...), custom_call_target="tpu_custom_call", output_to_operand_aliasing={{0}: (1, {}), {1}: (2, {})} | custom-call | tf_op jit(solution)/shard_map/advance_6/pallas_call | solution.py:339
  32.4 0.6 collective-permute-start.7
  33.0 3.5 %advance_7.3 = (f32[4,64,8192]{2,1,0:T(8,128)S(1)}, f32[8,8192]{1,0:T(8,128)S(1)}, bf16[4,4,512,256]{3,2,1,0:T(8,128)(2,1)S(1)}, f32[8,1024]{1,0:T(8,128)S(1)}, f32[520,128]{1,0:T(8,128)S(1)}) custom-call(s32[1]{0:T(128)} %bitcast.refs_0_, f32[4,64,8192]{2,1,0:T(8,128)S(1)} %get-tuple-element.126.refs_1_, ...), custom_call_target="tpu_custom_call", output_to_operand_aliasing={{0}: (1, {}), {1}: (2, {})} | custom-call | tf_op jit(solution)/shard_map/advance_7/pallas_call | solution.py:339
  36.5 1.6 %collective-permute-start.8 = (f32[520,128]{1,0:T(8,128)S(1)}, f32[520,128]{1,0:T(8,128)S(1)}, u32[]{:S(2)}, u32[]{:S(2)}) collective-permute-start(f32[520,128]{1,0:T(8,128)S(1)} %get-tuple-element.144), channel_id=1, source_target_pairs={{0,16},{16,0},{1,17},{17,1},{2,18},{18,2},{3,19},{19,3},{4,20},{20... | collective-permute-start | bytes 798728 | tf_op jit(solution)/shard_map/ppermute | solution.py:364
  38.1 3.5 %advance_0.3 = (f32[4,64,8192]{2,1,0:T(8,128)S(1)}, f32[8,8192]{1,0:T(8,128)S(1)}, bf16[4,4,512,256]{3,2,1,0:T(8,128)(2,1)S(1)}, f32[8,1024]{1,0:T(8,128)S(1)}, f32[520,128]{1,0:T(8,128)S(1)}) custom-call(s32[1]{0:T(128)} %bitcast.refs_0_, f32[4,64,8192]{2,1,0:T(8,128)S(1)} %get-tuple-element.129.refs_1_, ...), custom_call_target="tpu_custom_call", output_to_operand_aliasing={{0}: (1, {}), {1}: (2, {})} | custom-call | tf_op jit(solution)/shard_map/advance_0/pallas_call | solution.py:339
  41.7 0.6 collective-permute-start.9
  42.2 3.1 %advance_2.4 = (f32[4,64,8192]{2,1,0:T(8,128)S(1)}, f32[4,64,8192]{2,1,0:T(8,128)S(1)}, f32[8,8192]{1,0:T(8,128)S(1)}, f32[520,128]{1,0:T(8,128)S(1)}) custom-call(s32[1]{0:T(128)} %bitcast.refs_0_, f32[4,64,8192]{2,1,0:T(8,128)S(1)} %get-tuple-element.132.refs_1_, f32[8,8192]{1,0:T(8,128)S(1)} %get-tuple-element.133.refs_2_, ...), custom_call_target="tpu_custom_call", output_to_operand_aliasing={{0}: (1, {})} | custom-call | tf_op jit(solution)/shard_map/advance_2/pallas_call | solution.py:339
  45.3 1.6 %collective-permute-start.10 = (f32[520,128]{1,0:T(8,128)S(1)}, f32[520,128]{1,0:T(8,128)S(1)}, u32[]{:S(2)}, u32[]{:S(2)}) collective-permute-start(f32[520,128]{1,0:T(8,128)S(1)} %get-tuple-element.156), channel_id=1, source_target_pairs={{0,16},{16,0},{1,17},{17,1},{2,18},{18,2},{3,19},{19,3},{4,20},{20... | collective-permute-start | bytes 798728 | tf_op jit(solution)/shard_map/ppermute | solution.py:364
  46.9 2.8 %advance_3.4 = (f32[4,64,8192]{2,1,0:T(8,128)S(1)}, f32[4,64,8192]{2,1,0:T(8,128)S(1)}, f32[8,8192]{1,0:T(8,128)S(1)}, f32[520,128]{1,0:T(8,128)S(1)}) custom-call(s32[1]{0:T(128)} %bitcast.refs_0_, f32[4,64,8192]{2,1,0:T(8,128)S(1)} %get-tuple-element.135.refs_1_, ...), custom_call_target="tpu_custom_call", output_to_operand_aliasing={{0}: (1, {}), {1}: (3, {}), {2}: (4, {})} | custom-call | tf_op jit(solution)/shard_map/advance_3/pallas_call | solution.py:339
  49.7 0.6 collective-permute-start.12
  50.3 2.7 %advance_4.4 = (f32[4,64,8192]{2,1,0:T(8,128)S(1)}, f32[4,64,8192]{2,1,0:T(8,128)S(1)}, f32[8,8192]{1,0:T(8,128)S(1)}, f32[3,64,128]{2,1,0:T(8,128)S(1)}, f32[520,128]{1,0:T(8,128)S(1)}) custom-call(s32[1]{0:T(128)} %bitcast.refs_0_, f32[4,64,8192]{2,1,0:T(8,128)S(1)} %get-tuple-element.141.refs_1_, ...), custom_call_target="tpu_custom_call", output_to_operand_aliasing={{0}: (1, {}), {1}: (3, {}), {2}: (4, {})} | custom-call | tf_op jit(solution)/shard_map/advance_4/pallas_call | solution.py:339
  53.1 1.6 %collective-permute-start.14 = (f32[520,128]{1,0:T(8,128)S(1)}, f32[520,128]{1,0:T(8,128)S(1)}, u32[]{:S(2)}, u32[]{:S(2)}) collective-permute-start(f32[520,128]{1,0:T(8,128)S(1)} %get-tuple-element.168), channel_id=1, source_target_pairs={{0,16},{16,0},{1,17},{17,1},{2,18},{18,2},{3,19},{19,3},{4,20},{20... | collective-permute-start | bytes 798728 | tf_op jit(solution)/shard_map/ppermute | solution.py:364
  54.7 2.7 %advance_5.4 = (f32[4,64,8192]{2,1,0:T(8,128)S(1)}, f32[4,64,8192]{2,1,0:T(8,128)S(1)}, f32[8,8192]{1,0:T(8,128)S(1)}, f32[3,64,128]{2,1,0:T(8,128)S(1)}, f32[520,128]{1,0:T(8,128)S(1)}) custom-call(s32[1]{0:T(128)} %bitcast.refs_0_, f32[4,64,8192]{2,1,0:T(8,128)S(1)} %get-tuple-element.147.refs_1_, ...), custom_call_target="tpu_custom_call", output_to_operand_aliasing={{0}: (1, {}), {1}: (3, {}), {2}: (4, {})} | custom-call | tf_op jit(solution)/shard_map/advance_5/pallas_call | solution.py:339
  57.4 1.3 collective-permute-start.15
  58.6 1.2 collective-permute-done.11.refs_8_
  59.8 1.9 %collective-permute-start.13 = (f32[3,64,128]{2,1,0:T(8,128)S(1)}, f32[3,64,128]{2,1,0:T(8,128)S(1)}, u32[]{:S(2)}, u32[]{:S(2)}) collective-permute-start(f32[3,64,128]{2,1,0:T(8,128)S(1)} %get-tuple-element.165), channel_id=1, source_target_pairs={{1,0},{2,1},{3,2},{4,3},{5,4},{6,5},{7,6},{8,7},{9,8},{10,9},{11,1... | collective-permute-start | bytes 294920 | tf_op jit(solution)/shard_map/ppermute | solution.py:370
  61.8 2.6 %advance_0.4 = (f32[4,64,8192]{2,1,0:T(8,128)S(1)}, f32[8,8192]{1,0:T(8,128)S(1)}, f32[520,128]{1,0:T(8,128)S(1)}) custom-call(s32[1]{0:T(128)} %bitcast.refs_0_, f32[4,64,8192]{2,1,0:T(8,128)S(1)} %get-tuple-element.153.refs_1_, f32[8,8192]{1,0:T(8,128)S(1)} %get-tuple-element.133.refs_2_, ...), custom_call_target="tpu_custom_call", output_to_operand_aliasing={{0}: (3, {}), {1}: (4, {})} | custom-call | tf_op jit(solution)/shard_map/advance_0/pallas_call | solution.py:339
  64.4 1.6 %collective-permute-start.16 = (f32[520,128]{1,0:T(8,128)S(1)}, f32[520,128]{1,0:T(8,128)S(1)}, u32[]{:S(2)}, u32[]{:S(2)}) collective-permute-start(f32[520,128]{1,0:T(8,128)S(1)} %get-tuple-element.176), channel_id=1, source_target_pairs={{0,16},{16,0},{1,17},{17,1},{2,18},{18,2},{3,19},{19,3},{4,20},{20... | collective-permute-start | bytes 798728 | tf_op jit(solution)/shard_map/ppermute | solution.py:364
  66.0 2.6 %advance_7.4 = (f32[4,64,8192]{2,1,0:T(8,128)S(1)}, f32[8,8192]{1,0:T(8,128)S(1)}, f32[520,128]{1,0:T(8,128)S(1)}) custom-call(s32[1]{0:T(128)} %bitcast.refs_0_, f32[4,64,8192]{2,1,0:T(8,128)S(1)} %get-tuple-element.153.refs_1_, f32[8,8192]{1,0:T(8,128)S(1)} %get-tuple-element.133.refs_2_, ...), custom_call_target="tpu_custom_call", output_to_operand_aliasing={{0}: (3, {}), {1}: (4, {})} | custom-call | tf_op jit(solution)/shard_map/advance_7/pallas_call | solution.py:339
  68.7 1.3 collective-permute-start.17
  70.0 1.0 collective-permute-done.14.refs_5_
  70.9 2.6 %advance_6.4 = (f32[4,64,8192]{2,1,0:T(8,128)S(1)}, f32[8,8192]{1,0:T(8,128)S(1)}, f32[520,128]{1,0:T(8,128)S(1)}) custom-call(s32[1]{0:T(128)} %bitcast.refs_0_, f32[4,64,8192]{2,1,0:T(8,128)S(1)} %get-tuple-element.153.refs_1_, f32[8,8192]{1,0:T(8,128)S(1)} %get-tuple-element.133.refs_2_, ...), custom_call_target="tpu_custom_call", output_to_operand_aliasing={{0}: (3, {}), {1}: (4, {})} | custom-call | tf_op jit(solution)/shard_map/advance_6/pallas_call | solution.py:339
  73.6 2.1 %collective-permute-start.18 = (f32[520,128]{1,0:T(8,128)S(1)}, f32[520,128]{1,0:T(8,128)S(1)}, u32[]{:S(2)}, u32[]{:S(2)}) collective-permute-start(f32[520,128]{1,0:T(8,128)S(1)} %get-tuple-element.184), channel_id=1, source_target_pairs={{0,16},{16,0},{1,17},{17,1},{2,18},{18,2},{3,19},{19,3},{4,20},{20... | collective-permute-start | bytes 798728 | tf_op jit(solution)/shard_map/ppermute | solution.py:364
  75.7 1.0 collective-permute-done.15.refs_5_
  76.6 3.1 %advance_1.4 = (f32[4,64,8192]{2,1,0:T(8,128)S(1)}, f32[8,8192]{1,0:T(8,128)S(1)}, f32[520,128]{1,0:T(8,128)S(1)}) custom-call(s32[1]{0:T(128)} %bitcast.refs_0_, f32[4,64,8192]{2,1,0:T(8,128)S(1)} %get-tuple-element.153.refs_1_, f32[8,8192]{1,0:T(8,128)S(1)} %get-tuple-element.133.refs_2_, ...), custom_call_target="tpu_custom_call", output_to_operand_aliasing={{0}: (3, {}), {1}: (4, {})} | custom-call | tf_op jit(solution)/shard_map/advance_1/pallas_call | solution.py:339
  79.7 2.1 %collective-permute-start.20 = (f32[520,128]{1,0:T(8,128)S(1)}, f32[520,128]{1,0:T(8,128)S(1)}, u32[]{:S(2)}, u32[]{:S(2)}) collective-permute-start(f32[520,128]{1,0:T(8,128)S(1)} %get-tuple-element.189), channel_id=1, source_target_pairs={{0,16},{16,0},{1,17},{17,1},{2,18},{18,2},{3,19},{19,3},{4,20},{20... | collective-permute-start | bytes 798728 | tf_op jit(solution)/shard_map/ppermute | solution.py:364
  82.3 2.7 %advance_3.5 = (f32[4,64,8192]{2,1,0:T(8,128)S(1)}, f32[4,64,8192]{2,1,0:T(8,128)S(1)}, f32[8,8192]{1,0:T(8,128)S(1)}, f32[3,64,128]{2,1,0:T(8,128)S(1)}, f32[520,128]{1,0:T(8,128)S(1)}) custom-call(s32[1]{0:T(128)} %bitcast.refs_0_, f32[4,64,8192]{2,1,0:T(8,128)S(1)} %get-tuple-element.174.refs_1_, ...), custom_call_target="tpu_custom_call", output_to_operand_aliasing={{0}: (1, {})} | custom-call | tf_op jit(solution)/shard_map/advance_3/pallas_call | solution.py:339
  85.1 3.6 %collective-permute-start.19 = (f32[3,64,128]{2,1,0:T(8,128)S(1)}, f32[3,64,128]{2,1,0:T(8,128)S(1)}, u32[]{:S(2)}, u32[]{:S(2)}) collective-permute-start(f32[3,64,128]{2,1,0:T(8,128)S(1)} %get-tuple-element.185), channel_id=1, source_target_pairs={{1,0},{2,1},{3,2},{4,3},{5,4},{6,5},{7,6},{8,7},{9,8},{10,9},{11,1... | collective-permute-start | bytes 294920 | tf_op jit(solution)/shard_map/ppermute | solution.py:370
  88.7 2.7 %advance_4.5 = (f32[4,64,8192]{2,1,0:T(8,128)S(1)}, f32[4,64,8192]{2,1,0:T(8,128)S(1)}, f32[8,8192]{1,0:T(8,128)S(1)}, f32[3,64,128]{2,1,0:T(8,128)S(1)}, f32[520,128]{1,0:T(8,128)S(1)}) custom-call(s32[1]{0:T(128)} %bitcast.refs_0_, f32[4,64,8192]{2,1,0:T(8,128)S(1)} %get-tuple-element.177.refs_1_, ...), custom_call_target="tpu_custom_call", output_to_operand_aliasing={{0}: (1, {}), {1}: (3, {}), {2}: (4, {})} | custom-call | tf_op jit(solution)/shard_map/advance_4/pallas_call | solution.py:339
  91.5 1.6 %collective-permute-start.22 = (f32[520,128]{1,0:T(8,128)S(1)}, f32[520,128]{1,0:T(8,128)S(1)}, u32[]{:S(2)}, u32[]{:S(2)}) collective-permute-start(f32[520,128]{1,0:T(8,128)S(1)} %get-tuple-element.194), channel_id=1, source_target_pairs={{0,16},{16,0},{1,17},{17,1},{2,18},{18,2},{3,19},{19,3},{4,20},{20... | collective-permute-start | bytes 798728 | tf_op jit(solution)/shard_map/ppermute | solution.py:364
  93.1 0.7 collective-permute-done.18.refs_5_
  93.8 2.0 %collective-permute-start.23 = (f32[520,128]{1,0:T(8,128)S(1)}, f32[520,128]{1,0:T(8,128)S(1)}, u32[]{:S(2)}, u32[]{:S(2)}) collective-permute-start(f32[520,128]{1,0:T(8,128)S(1)} %get-tuple-element.197), channel_id=1, source_target_pairs={{0,16},{16,0},{1,17},{17,1},{2,18},{18,2},{3,19},{19,3},{4,20},{20... | collective-permute-start | bytes 798728 | tf_op jit(solution)/shard_map/ppermute | solution.py:364
  95.8 3.0 %advance_7.5 = (f32[4,64,8192]{2,1,0:T(8,128)S(1)}, f32[4,64,8192]{2,1,0:T(8,128)S(1)}, f32[8,8192]{1,0:T(8,128)S(1)}, f32[520,128]{1,0:T(8,128)S(1)}) custom-call(s32[1]{0:T(128)} %bitcast.refs_0_, f32[4,64,8192]{2,1,0:T(8,128)S(1)} %get-tuple-element.181.refs_1_, ...), custom_call_target="tpu_custom_call", output_to_operand_aliasing={{0}: (1, {}), {1}: (3, {}), {2}: (4, {})} | custom-call | tf_op jit(solution)/shard_map/advance_7/pallas_call | solution.py:339
  98.9 0.6 collective-permute-done.20.refs_5_
  99.5 2.7 %advance_0.5 = (f32[4,64,8192]{2,1,0:T(8,128)S(1)}, f32[4,64,8192]{2,1,0:T(8,128)S(1)}, f32[8,8192]{1,0:T(8,128)S(1)}, f32[520,128]{1,0:T(8,128)S(1)}) custom-call(s32[1]{0:T(128)} %bitcast.refs_0_, f32[4,64,8192]{2,1,0:T(8,128)S(1)} %get-tuple-element.186.refs_1_, ...), custom_call_target="tpu_custom_call", output_to_operand_aliasing={{0}: (1, {}), {1}: (3, {}), {2}: (4, {})} | custom-call | tf_op jit(solution)/shard_map/advance_0/pallas_call | solution.py:339
  102.2 2.1 %collective-permute-start.25 = (f32[520,128]{1,0:T(8,128)S(1)}, f32[520,128]{1,0:T(8,128)S(1)}, u32[]{:S(2)}, u32[]{:S(2)}) collective-permute-start(f32[520,128]{1,0:T(8,128)S(1)} %get-tuple-element.205), channel_id=1, source_target_pairs={{0,16},{16,0},{1,17},{17,1},{2,18},{18,2},{3,19},{19,3},{4,20},{20... | collective-permute-start | bytes 798728 | tf_op jit(solution)/shard_map/ppermute | solution.py:364
  104.3 0.9 collective-permute-done.22.refs_5_
  105.2 2.6 %advance_5.5 = (f32[4,64,8192]{2,1,0:T(8,128)S(1)}, f32[8,8192]{1,0:T(8,128)S(1)}, f32[4,64,8192]{2,1,0:T(8,128)}, f32[520,128]{1,0:T(8,128)S(1)}) custom-call(s32[1]{0:T(128)} %bitcast.refs_0_, f32[4,64,8192]{2,1,0:T(8,128)S(1)} %get-tuple-element.191.refs_1_, ...), custom_call_target="tpu_custom_call", output_to_operand_aliasing={{0}: (3, {}), {1}: (4, {})} | custom-call | tf_op jit(solution)/shard_map/advance_5/pallas_call | solution.py:339
  107.8 2.1 %collective-permute-start.26 = (f32[520,128]{1,0:T(8,128)S(1)}, f32[520,128]{1,0:T(8,128)S(1)}, u32[]{:S(2)}, u32[]{:S(2)}) collective-permute-start(f32[520,128]{1,0:T(8,128)S(1)} %get-tuple-element.209), channel_id=1, source_target_pairs={{0,16},{16,0},{1,17},{17,1},{2,18},{18,2},{3,19},{19,3},{4,20},{20... | collective-permute-start | bytes 798728 | tf_op jit(solution)/shard_map/ppermute | solution.py:364
  109.9 1.0 collective-permute-done.23.refs_5_
  110.9 2.6 %advance_6.5 = (f32[4,64,8192]{2,1,0:T(8,128)S(1)}, f32[8,8192]{1,0:T(8,128)S(1)}, f32[4,64,8192]{2,1,0:T(8,128)}, f32[520,128]{1,0:T(8,128)S(1)}) custom-call(s32[1]{0:T(128)} %bitcast.refs_0_, f32[4,64,8192]{2,1,0:T(8,128)S(1)} %get-tuple-element.191.refs_1_, ...), custom_call_target="tpu_custom_call", output_to_operand_aliasing={{0}: (3, {}), {1}: (4, {}), {2}: (6, {})} | custom-call | tf_op jit(solution)/shard_map/advance_6/pallas_call | solution.py:339
  113.5 2.1 %collective-permute-start.27 = (f32[520,128]{1,0:T(8,128)S(1)}, f32[520,128]{1,0:T(8,128)S(1)}, u32[]{:S(2)}, u32[]{:S(2)}) collective-permute-start(f32[520,128]{1,0:T(8,128)S(1)} %get-tuple-element.212), channel_id=1, source_target_pairs={{0,16},{16,0},{1,17},{17,1},{2,18},{18,2},{3,19},{19,3},{4,20},{20... | collective-permute-start | bytes 798728 | tf_op jit(solution)/shard_map/ppermute | solution.py:364
  115.6 1.0 collective-permute-done.24.refs_5_
  116.6 3.1 %advance_1.5 = (f32[4,64,8192]{2,1,0:T(8,128)S(1)}, f32[8,8192]{1,0:T(8,128)S(1)}, f32[4,64,8192]{2,1,0:T(8,128)}, f32[520,128]{1,0:T(8,128)S(1)}) custom-call(s32[1]{0:T(128)} %bitcast.refs_0_, f32[4,64,8192]{2,1,0:T(8,128)S(1)} %get-tuple-element.191.refs_1_, ...), custom_call_target="tpu_custom_call", output_to_operand_aliasing={{0}: (3, {}), {1}: (4, {}), {2}: (6, {})} | custom-call | tf_op jit(solution)/shard_map/advance_1/pallas_call | solution.py:339
  119.7 2.1 %collective-permute-start.28 = (f32[520,128]{1,0:T(8,128)S(1)}, f32[520,128]{1,0:T(8,128)S(1)}, u32[]{:S(2)}, u32[]{:S(2)}) collective-permute-start(f32[520,128]{1,0:T(8,128)S(1)} %get-tuple-element.215), channel_id=1, source_target_pairs={{0,16},{16,0},{1,17},{17,1},{2,18},{18,2},{3,19},{19,3},{4,20},{20... | collective-permute-start | bytes 798728 | tf_op jit(solution)/shard_map/ppermute | solution.py:364
  122.3 3.1 %advance_2.5 = (f32[4,64,8192]{2,1,0:T(8,128)S(1)}, f32[8,8192]{1,0:T(8,128)S(1)}, f32[4,64,8192]{2,1,0:T(8,128)}, f32[520,128]{1,0:T(8,128)S(1)}) custom-call(s32[1]{0:T(128)} %bitcast.refs_0_, f32[4,64,8192]{2,1,0:T(8,128)S(1)} %get-tuple-element.191.refs_1_, ...), custom_call_target="tpu_custom_call", output_to_operand_aliasing={{0}: (3, {}), {1}: (4, {}), {2}: (6, {})} | custom-call | tf_op jit(solution)/shard_map/advance_2/pallas_call | solution.py:339
  125.4 2.1 %collective-permute-start.29 = (f32[520,128]{1,0:T(8,128)S(1)}, f32[520,128]{1,0:T(8,128)S(1)}, u32[]{:S(2)}, u32[]{:S(2)}) collective-permute-start(f32[520,128]{1,0:T(8,128)S(1)} %get-tuple-element.218), channel_id=1, source_target_pairs={{0,16},{16,0},{1,17},{17,1},{2,18},{18,2},{3,19},{19,3},{4,20},{20... | collective-permute-start | bytes 798728 | tf_op jit(solution)/shard_map/ppermute | solution.py:364
  128.0 1.0 complete.4
  129.0 4.7 %collective-permute-done.27.refs_3_ = f32[520,128]{1,0:T(8,128)S(1)} collective-permute-done((f32[520,128]{1,0:T(8,128)S(1)}, f32[520,128]{1,0:T(8,128)S(1)}, u32[]{:S(2)}, u32[]{:S(2)}) %collective-permute-start.27) | collective-permute-done | bytes 266272 | tf_op jit(solution)/shard_map/ppermute | solution.py:364
  133.7 1.0 complete.5
  134.7 4.7 %collective-permute-done.28.refs_3_ = f32[520,128]{1,0:T(8,128)S(1)} collective-permute-done((f32[520,128]{1,0:T(8,128)S(1)}, f32[520,128]{1,0:T(8,128)S(1)}, u32[]{:S(2)}, u32[]{:S(2)}) %collective-permute-start.28) | collective-permute-done | bytes 266272 | tf_op jit(solution)/shard_map/ppermute | solution.py:364
  139.4 1.0 complete.6
  140.4 3.8 %collective-permute-done.29.refs_3_ = f32[520,128]{1,0:T(8,128)S(1)} collective-permute-done((f32[520,128]{1,0:T(8,128)S(1)}, f32[520,128]{1,0:T(8,128)S(1)}, u32[]{:S(2)}, u32[]{:S(2)}) %collective-permute-start.29) | collective-permute-done | bytes 266272 | tf_op jit(solution)/shard_map/ppermute | solution.py:364
  144.3 1.0 complete.7
  (25 shorter events, 2.1 us)
Async XLA Ops:
  3.6 12.1 %collective-permute-start = (f32[520,128]{1,0:T(8,128)S(1)}, f32[520,128]{1,0:T(8,128)S(1)}, u32[]{:S(2)}, u32[]{:S(2)}) collective-permute-start(f32[520,128]{1,0:T(8,128)S(1)} %get-tuple-element.120), channel_id=1, source_target_pairs={{0,16},{16,0},{1,17},{17,1},{2,18},{18,2},{3,19},{19,3},{4,20},{20... | collective-permute-start | bytes 798728 | tf_op jit(solution)/shard_map/ppermute | solution.py:364
  10.1 17.2 %collective-permute-start.1 = (f32[520,128]{1,0:T(8,128)S(1)}, f32[520,128]{1,0:T(8,128)S(1)}, u32[]{:S(2)}, u32[]{:S(2)}) collective-permute-start(f32[520,128]{1,0:T(8,128)S(1)} %get-tuple-element.125), channel_id=1, source_target_pairs={{0,16},{16,0},{1,17},{17,1},{2,18},{18,2},{3,19},{19,3},{4,20},{20... | collective-permute-start | bytes 798728 | tf_op jit(solution)/shard_map/ppermute | solution.py:364
  13.7 19.3 %collective-permute-start.2 = (f32[520,128]{1,0:T(8,128)S(1)}, f32[520,128]{1,0:T(8,128)S(1)}, u32[]{:S(2)}, u32[]{:S(2)}) collective-permute-start(f32[520,128]{1,0:T(8,128)S(1)} %get-tuple-element.128), channel_id=1, source_target_pairs={{0,16},{16,0},{1,17},{17,1},{2,18},{18,2},{3,19},{19,3},{4,20},{20... | collective-permute-start | bytes 798728 | tf_op jit(solution)/shard_map/ppermute | solution.py:364
  19.3 18.8 %collective-permute-start.5 = (f32[520,128]{1,0:T(8,128)S(1)}, f32[520,128]{1,0:T(8,128)S(1)}, u32[]{:S(2)}, u32[]{:S(2)}) collective-permute-start(f32[520,128]{1,0:T(8,128)S(1)} %get-tuple-element.131), channel_id=1, source_target_pairs={{0,16},{16,0},{1,17},{17,1},{2,18},{18,2},{3,19},{19,3},{4,20},{20... | collective-permute-start | bytes 798728 | tf_op jit(solution)/shard_map/ppermute | solution.py:364
  20.5 11.9 %collective-permute-start.4 = (f32[3,64,128]{2,1,0:T(8,128)S(1)}, f32[3,64,128]{2,1,0:T(8,128)S(1)}, u32[]{:S(2)}, u32[]{:S(2)}) collective-permute-start(f32[3,64,128]{2,1,0:T(8,128)S(1)} %get-tuple-element.221), channel_id=1, source_target_pairs={{1,0},{2,1},{3,2},{4,3},{5,4},{6,5},{7,6},{8,7},{9,8},{10,9},{11,1... | collective-permute-start | bytes 294920 | tf_op jit(solution)/shard_map/ppermute | solution.py:370
  23.7 9.3 %collective-permute-start.3 = (f32[3,64,128]{2,1,0:T(8,128)S(1)}, f32[3,64,128]{2,1,0:T(8,128)S(1)}, u32[]{:S(2)}, u32[]{:S(2)}) collective-permute-start(f32[3,64,128]{2,1,0:T(8,128)S(1)} %get-tuple-element.222), channel_id=1, source_target_pairs={{0,1},{1,2},{2,3},{3,4},{4,5},{5,6},{6,7},{7,8},{8,9},{9,10},{10,1... | collective-permute-start | bytes 294920 | tf_op jit(solution)/shard_map/ppermute | solution.py:367
  27.3 14.9 %collective-permute-start.6 = (f32[520,128]{1,0:T(8,128)S(1)}, f32[520,128]{1,0:T(8,128)S(1)}, u32[]{:S(2)}, u32[]{:S(2)}) collective-permute-start(f32[520,128]{1,0:T(8,128)S(1)} %get-tuple-element.134), channel_id=1, source_target_pairs={{0,16},{16,0},{1,17},{17,1},{2,18},{18,2},{3,19},{19,3},{4,20},{20... | collective-permute-start | bytes 798728 | tf_op jit(solution)/shard_map/ppermute | solution.py:364
  32.4 14.4 %collective-permute-start.7 = (f32[520,128]{1,0:T(8,128)S(1)}, f32[520,128]{1,0:T(8,128)S(1)}, u32[]{:S(2)}, u32[]{:S(2)}) collective-permute-start(f32[520,128]{1,0:T(8,128)S(1)} %get-tuple-element.138), channel_id=1, source_target_pairs={{0,16},{16,0},{1,17},{17,1},{2,18},{18,2},{3,19},{19,3},{4,20},{20... | collective-permute-start | bytes 798728 | tf_op jit(solution)/shard_map/ppermute | solution.py:364
  36.5 13.8 %collective-permute-start.8 = (f32[520,128]{1,0:T(8,128)S(1)}, f32[520,128]{1,0:T(8,128)S(1)}, u32[]{:S(2)}, u32[]{:S(2)}) collective-permute-start(f32[520,128]{1,0:T(8,128)S(1)} %get-tuple-element.144), channel_id=1, source_target_pairs={{0,16},{16,0},{1,17},{17,1},{2,18},{18,2},{3,19},{19,3},{4,20},{20... | collective-permute-start | bytes 798728 | tf_op jit(solution)/shard_map/ppermute | solution.py:364
  41.7 13.0 %collective-permute-start.9 = (f32[520,128]{1,0:T(8,128)S(1)}, f32[520,128]{1,0:T(8,128)S(1)}, u32[]{:S(2)}, u32[]{:S(2)}) collective-permute-start(f32[520,128]{1,0:T(8,128)S(1)} %get-tuple-element.150), channel_id=1, source_target_pairs={{0,16},{16,0},{1,17},{17,1},{2,18},{18,2},{3,19},{19,3},{4,20},{20... | collective-permute-start | bytes 798728 | tf_op jit(solution)/shard_map/ppermute | solution.py:364
  45.3 16.5 %collective-permute-start.10 = (f32[520,128]{1,0:T(8,128)S(1)}, f32[520,128]{1,0:T(8,128)S(1)}, u32[]{:S(2)}, u32[]{:S(2)}) collective-permute-start(f32[520,128]{1,0:T(8,128)S(1)} %get-tuple-element.156), channel_id=1, source_target_pairs={{0,16},{16,0},{1,17},{17,1},{2,18},{18,2},{3,19},{19,3},{4,20},{20... | collective-permute-start | bytes 798728 | tf_op jit(solution)/shard_map/ppermute | solution.py:364
  49.7 16.3 %collective-permute-start.12 = (f32[520,128]{1,0:T(8,128)S(1)}, f32[520,128]{1,0:T(8,128)S(1)}, u32[]{:S(2)}, u32[]{:S(2)}) collective-permute-start(f32[520,128]{1,0:T(8,128)S(1)} %get-tuple-element.162), channel_id=1, source_target_pairs={{0,16},{16,0},{1,17},{17,1},{2,18},{18,2},{3,19},{19,3},{4,20},{20... | collective-permute-start | bytes 798728 | tf_op jit(solution)/shard_map/ppermute | solution.py:364
  53.0 6.8 %collective-permute-start.11 = (f32[3,64,128]{2,1,0:T(8,128)S(1)}, f32[3,64,128]{2,1,0:T(8,128)S(1)}, u32[]{:S(2)}, u32[]{:S(2)}) collective-permute-start(f32[3,64,128]{2,1,0:T(8,128)S(1)} %get-tuple-element.159), channel_id=1, source_target_pairs={{0,1},{1,2},{2,3},{3,4},{4,5},{5,6},{6,7},{7,8},{8,9},{9,10},{10,1... | collective-permute-start | bytes 294920 | tf_op jit(solution)/shard_map/ppermute | solution.py:367
  53.1 17.9 %collective-permute-start.14 = (f32[520,128]{1,0:T(8,128)S(1)}, f32[520,128]{1,0:T(8,128)S(1)}, u32[]{:S(2)}, u32[]{:S(2)}) collective-permute-start(f32[520,128]{1,0:T(8,128)S(1)} %get-tuple-element.168), channel_id=1, source_target_pairs={{0,16},{16,0},{1,17},{17,1},{2,18},{18,2},{3,19},{19,3},{4,20},{20... | collective-permute-start | bytes 798728 | tf_op jit(solution)/shard_map/ppermute | solution.py:364
  57.4 19.3 %collective-permute-start.15 = (f32[520,128]{1,0:T(8,128)S(1)}, f32[520,128]{1,0:T(8,128)S(1)}, u32[]{:S(2)}, u32[]{:S(2)}) collective-permute-start(f32[520,128]{1,0:T(8,128)S(1)} %get-tuple-element.173), channel_id=1, source_target_pairs={{0,16},{16,0},{1,17},{17,1},{2,18},{18,2},{3,19},{19,3},{4,20},{20... | collective-permute-start | bytes 798728 | tf_op jit(solution)/shard_map/ppermute | solution.py:364
  59.8 6.2 %collective-permute-start.13 = (f32[3,64,128]{2,1,0:T(8,128)S(1)}, f32[3,64,128]{2,1,0:T(8,128)S(1)}, u32[]{:S(2)}, u32[]{:S(2)}) collective-permute-start(f32[3,64,128]{2,1,0:T(8,128)S(1)} %get-tuple-element.165), channel_id=1, source_target_pairs={{1,0},{2,1},{3,2},{4,3},{5,4},{6,5},{7,6},{8,7},{9,8},{10,9},{11,1... | collective-permute-start | bytes 294920 | tf_op jit(solution)/shard_map/ppermute | solution.py:370
  64.4 17.9 %collective-permute-start.16 = (f32[520,128]{1,0:T(8,128)S(1)}, f32[520,128]{1,0:T(8,128)S(1)}, u32[]{:S(2)}, u32[]{:S(2)}) collective-permute-start(f32[520,128]{1,0:T(8,128)S(1)} %get-tuple-element.176), channel_id=1, source_target_pairs={{0,16},{16,0},{1,17},{17,1},{2,18},{18,2},{3,19},{19,3},{4,20},{20... | collective-permute-start | bytes 798728 | tf_op jit(solution)/shard_map/ppermute | solution.py:364
  68.7 20.0 %collective-permute-start.17 = (f32[520,128]{1,0:T(8,128)S(1)}, f32[520,128]{1,0:T(8,128)S(1)}, u32[]{:S(2)}, u32[]{:S(2)}) collective-permute-start(f32[520,128]{1,0:T(8,128)S(1)} %get-tuple-element.180), channel_id=1, source_target_pairs={{0,16},{16,0},{1,17},{17,1},{2,18},{18,2},{3,19},{19,3},{4,20},{20... | collective-permute-start | bytes 798728 | tf_op jit(solution)/shard_map/ppermute | solution.py:364
  73.6 20.2 %collective-permute-start.18 = (f32[520,128]{1,0:T(8,128)S(1)}, f32[520,128]{1,0:T(8,128)S(1)}, u32[]{:S(2)}, u32[]{:S(2)}) collective-permute-start(f32[520,128]{1,0:T(8,128)S(1)} %get-tuple-element.184), channel_id=1, source_target_pairs={{0,16},{16,0},{1,17},{17,1},{2,18},{18,2},{3,19},{19,3},{4,20},{20... | collective-permute-start | bytes 798728 | tf_op jit(solution)/shard_map/ppermute | solution.py:364
  79.7 19.8 %collective-permute-start.20 = (f32[520,128]{1,0:T(8,128)S(1)}, f32[520,128]{1,0:T(8,128)S(1)}, u32[]{:S(2)}, u32[]{:S(2)}) collective-permute-start(f32[520,128]{1,0:T(8,128)S(1)} %get-tuple-element.189), channel_id=1, source_target_pairs={{0,16},{16,0},{1,17},{17,1},{2,18},{18,2},{3,19},{19,3},{4,20},{20... | collective-permute-start | bytes 798728 | tf_op jit(solution)/shard_map/ppermute | solution.py:364
  85.1 10.7 %collective-permute-start.19 = (f32[3,64,128]{2,1,0:T(8,128)S(1)}, f32[3,64,128]{2,1,0:T(8,128)S(1)}, u32[]{:S(2)}, u32[]{:S(2)}) collective-permute-start(f32[3,64,128]{2,1,0:T(8,128)S(1)} %get-tuple-element.185), channel_id=1, source_target_pairs={{1,0},{2,1},{3,2},{4,3},{5,4},{6,5},{7,6},{8,7},{9,8},{10,9},{11,1... | collective-permute-start | bytes 294920 | tf_op jit(solution)/shard_map/ppermute | solution.py:370
  91.4 7.4 %collective-permute-start.21 = (f32[3,64,128]{2,1,0:T(8,128)S(1)}, f32[3,64,128]{2,1,0:T(8,128)S(1)}, u32[]{:S(2)}, u32[]{:S(2)}) collective-permute-start(f32[3,64,128]{2,1,0:T(8,128)S(1)} %get-tuple-element.190), channel_id=1, source_target_pairs={{0,1},{1,2},{2,3},{3,4},{4,5},{5,6},{6,7},{7,8},{8,9},{9,10},{10,1... | collective-permute-start | bytes 294920 | tf_op jit(solution)/shard_map/ppermute | solution.py:367
  91.5 13.7 %collective-permute-start.22 = (f32[520,128]{1,0:T(8,128)S(1)}, f32[520,128]{1,0:T(8,128)S(1)}, u32[]{:S(2)}, u32[]{:S(2)}) collective-permute-start(f32[520,128]{1,0:T(8,128)S(1)} %get-tuple-element.194), channel_id=1, source_target_pairs={{0,16},{16,0},{1,17},{17,1},{2,18},{18,2},{3,19},{19,3},{4,20},{20... | collective-permute-start | bytes 798728 | tf_op jit(solution)/shard_map/ppermute | solution.py:364
  93.8 17.1 %collective-permute-start.23 = (f32[520,128]{1,0:T(8,128)S(1)}, f32[520,128]{1,0:T(8,128)S(1)}, u32[]{:S(2)}, u32[]{:S(2)}) collective-permute-start(f32[520,128]{1,0:T(8,128)S(1)} %get-tuple-element.197), channel_id=1, source_target_pairs={{0,16},{16,0},{1,17},{17,1},{2,18},{18,2},{3,19},{19,3},{4,20},{20... | collective-permute-start | bytes 798728 | tf_op jit(solution)/shard_map/ppermute | solution.py:364
  98.8 17.8 %collective-permute-start.24 = (f32[520,128]{1,0:T(8,128)S(1)}, f32[520,128]{1,0:T(8,128)S(1)}, u32[]{:S(2)}, u32[]{:S(2)}) collective-permute-start(f32[520,128]{1,0:T(8,128)S(1)} %get-tuple-element.201), channel_id=1, source_target_pairs={{0,16},{16,0},{1,17},{17,1},{2,18},{18,2},{3,19},{19,3},{4,20},{20... | collective-permute-start | bytes 798728 | tf_op jit(solution)/shard_map/ppermute | solution.py:364
  102.2 20.1 %collective-permute-start.25 = (f32[520,128]{1,0:T(8,128)S(1)}, f32[520,128]{1,0:T(8,128)S(1)}, u32[]{:S(2)}, u32[]{:S(2)}) collective-permute-start(f32[520,128]{1,0:T(8,128)S(1)} %get-tuple-element.205), channel_id=1, source_target_pairs={{0,16},{16,0},{1,17},{17,1},{2,18},{18,2},{3,19},{19,3},{4,20},{20... | collective-permute-start | bytes 798728 | tf_op jit(solution)/shard_map/ppermute | solution.py:364
  107.8 20.2 %collective-permute-start.26 = (f32[520,128]{1,0:T(8,128)S(1)}, f32[520,128]{1,0:T(8,128)S(1)}, u32[]{:S(2)}, u32[]{:S(2)}) collective-permute-start(f32[520,128]{1,0:T(8,128)S(1)} %get-tuple-element.209), channel_id=1, source_target_pairs={{0,16},{16,0},{1,17},{17,1},{2,18},{18,2},{3,19},{19,3},{4,20},{20... | collective-permute-start | bytes 798728 | tf_op jit(solution)/shard_map/ppermute | solution.py:364
  113.5 20.2 %collective-permute-start.27 = (f32[520,128]{1,0:T(8,128)S(1)}, f32[520,128]{1,0:T(8,128)S(1)}, u32[]{:S(2)}, u32[]{:S(2)}) collective-permute-start(f32[520,128]{1,0:T(8,128)S(1)} %get-tuple-element.212), channel_id=1, source_target_pairs={{0,16},{16,0},{1,17},{17,1},{2,18},{18,2},{3,19},{19,3},{4,20},{20... | collective-permute-start | bytes 798728 | tf_op jit(solution)/shard_map/ppermute | solution.py:364
  119.7 19.7 %collective-permute-start.28 = (f32[520,128]{1,0:T(8,128)S(1)}, f32[520,128]{1,0:T(8,128)S(1)}, u32[]{:S(2)}, u32[]{:S(2)}) collective-permute-start(f32[520,128]{1,0:T(8,128)S(1)} %get-tuple-element.215), channel_id=1, source_target_pairs={{0,16},{16,0},{1,17},{17,1},{2,18},{18,2},{3,19},{19,3},{4,20},{20... | collective-permute-start | bytes 798728 | tf_op jit(solution)/shard_map/ppermute | solution.py:364
  125.4 18.9 %collective-permute-start.29 = (f32[520,128]{1,0:T(8,128)S(1)}, f32[520,128]{1,0:T(8,128)S(1)}, u32[]{:S(2)}, u32[]{:S(2)}) collective-permute-start(f32[520,128]{1,0:T(8,128)S(1)} %get-tuple-element.218), channel_id=1, source_target_pairs={{0,16},{16,0},{1,17},{17,1},{2,18},{18,2},{3,19},{19,3},{4,20},{20... | collective-permute-start | bytes 798728 | tf_op jit(solution)/shard_map/ppermute | solution.py:364
